TPU v7x, 32 devices: a whole 2x2x4 slice. The times are simulated.
32 devices in a mesh: ctx: 8 (over z, y), fsdp: 4 (over x, core).
Axes of the slice: x: 2, y: 2, z: 4, core: 2. Of those that a mesh axis runs over, the one named last changes fastest.
Arguments:
- tokens: bfloat16 [4, 1024, 640], P('fsdp', 'ctx'), may hold values from -8 to 8
- positions: int32 [4, 1024], P('fsdp'), may hold values from 0 to 1023, as said below
- qkv_weight: bfloat16 [640, 1536], P('fsdp'), may hold values from -1 to 1
- out_weight: bfloat16 [1024, 640], P('fsdp'), may hold values from -0.1875 to 0.1875
- gate_up_weight: bfloat16 [640, 4096], P('fsdp'), may hold values from -0.25 to 0.25
- down_weight: bfloat16 [2048, 640], P('fsdp'), may hold values from -0.125 to 0.125
- norm_gains: float32 [4, 640], replicated, may hold values from -0.5 to 0.5
- qk_gains: float32 [2, 256], replicated, may hold values from -0.5 to 0.5
- cotangent: bfloat16 [4, 1024, 640], P('fsdp', 'ctx'), may hold values from -6 to 6
Outputs:
- output: float32 [4, 1024, 640], P('fsdp', 'ctx')
- grad_tokens: float32 [4, 1024, 640], P('fsdp', 'ctx')
- grad_qkv: float32 [640, 1536], P('fsdp')
- grad_out: float32 [1024, 640], P('fsdp')
- grad_gate_up: float32 [640, 4096], P('fsdp')
- grad_down: float32 [2048, 640], P('fsdp')
- grad_norm_gains: float32 [4, 640], replicated
- grad_qk_gains: float32 [2, 256], replicated
Inputs may be any that keep to these rules, and one draw needn't show every extreme that they name: In every sequence each position 0 to 1023 occurs once. Each device's 2 * 64 stored tokens along ctx are two whole blocks of 64 consecutive positions starting at multiples of 64: block b and block 2 * 8 - 1 - b, in either order.
All inputs are finite; a program needn't handle non-finite values.
Results may differ from a plain program's by a relative error of at most 0.018.
Values may be sent and summed in bfloat16 or wider, within the bound.
A program may use at most 128 MiB of HBM per device.

v0:
```python
import math

import jax
import jax.numpy as jnp
from jax import lax
from jax.sharding import PartitionSpec as P

EPS = 1e-06
ROPE_BASE = 1000000.0
NEG = -1e30


def rms_forward(entries, weight):
    inv_rms = lax.rsqrt(jnp.mean(entries * entries, axis=-1, keepdims=True) + EPS)
    return (entries * inv_rms * (1.0 + weight), inv_rms)


def rms_backward(entries, inv_rms, weight, incoming):
    normed = entries * inv_rms
    scaled = incoming * (1.0 + weight)
    lead_axes = tuple(range(incoming.ndim - 1))
    d_weight = jnp.sum(incoming * normed, axis=lead_axes)
    d_entries = inv_rms * (scaled - normed * jnp.mean(scaled * normed, axis=-1, keepdims=True))
    return (d_entries, d_weight)


def rope_tables(places, head_size):
    half_size = head_size // 2
    frequency = ROPE_BASE ** (-2.0 * jnp.arange(half_size, dtype=jnp.float32) / head_size)
    angles = places.astype(jnp.float32)[:, None] * frequency[None, :]
    cosine = jnp.cos(angles)
    sine_part = jnp.sin(angles)
    return (jnp.concatenate([cosine, cosine], -1), jnp.concatenate([sine_part, sine_part], -1))


def rotate(entries, cosine, sine_part):
    half_size = entries.shape[-1] // 2
    turned = jnp.concatenate([-entries[..., half_size:], entries[..., :half_size]], -1)
    return entries * cosine + turned * sine_part


def gelu_tanh(entries):
    return jax.nn.gelu(entries, approximate=True)


def tile_scores(query_rows, query_places, key_sorted, tile_start, tile_size):
    key_tile = lax.dynamic_slice_in_dim(key_sorted, tile_start, tile_size, 0)
    scores = lax.dot_general(
        query_rows, key_tile, (((1,), (1,)), ((), ())), preferred_element_type=jnp.float32
    )
    key_places = tile_start + jnp.arange(tile_size, dtype=jnp.int32)
    return jnp.where(key_places[None, :] <= query_places[:, None], scores, NEG)


def attend_forward(query_rows, query_places, key_sorted, value_sorted):
    row_count, head_size = query_rows.shape
    length = key_sorted.shape[0]
    tile_size = math.gcd(length, 512)
    tile_limit = jnp.max(query_places) // tile_size + 1

    def total_step(tile_index, state):
        row_peak, row_total = state
        scores = tile_scores(
            query_rows, query_places, key_sorted, tile_index * tile_size, tile_size
        )
        new_peak = jnp.maximum(row_peak, jnp.max(scores, axis=1))
        row_total = row_total * jnp.exp(row_peak - new_peak) + jnp.sum(
            jnp.exp(scores - new_peak[:, None]), axis=1
        )
        return (new_peak, row_total)

    start_totals = (jnp.full((row_count,), NEG, jnp.float32), jnp.zeros((row_count,), jnp.float32))
    row_peak, row_total = lax.fori_loop(0, tile_limit, total_step, start_totals)
    log_total = row_peak + jnp.log(row_total)

    def mix_step(tile_index, weighted):
        tile_start = tile_index * tile_size
        scores = tile_scores(query_rows, query_places, key_sorted, tile_start, tile_size)
        value_tile = lax.dynamic_slice_in_dim(value_sorted, tile_start, tile_size, 0)
        weights_b = jnp.exp(scores - log_total[:, None]).astype(jnp.bfloat16)
        return weighted + jnp.dot(weights_b, value_tile, preferred_element_type=jnp.float32)

    weighted = lax.fori_loop(
        0, tile_limit, mix_step, jnp.zeros((row_count, head_size), jnp.float32)
    )
    return (weighted, log_total)


def attend_backward(
    query_rows,
    query_places,
    grad_rows,
    log_total,
    row_delta,
    key_sorted,
    value_sorted,
    key_grad,
    value_grad,
):
    row_count, head_size = query_rows.shape
    length = key_sorted.shape[0]
    tile_size = math.gcd(length, 512)
    tile_limit = jnp.max(query_places) // tile_size + 1

    def tile_step(tile_index, state):
        query_grad, key_acc, value_acc = state
        tile_start = tile_index * tile_size
        key_tile = lax.dynamic_slice_in_dim(key_sorted, tile_start, tile_size, 0)
        value_tile = lax.dynamic_slice_in_dim(value_sorted, tile_start, tile_size, 0)
        scores = tile_scores(query_rows, query_places, key_sorted, tile_start, tile_size)
        probs_f = jnp.exp(scores - log_total[:, None])
        probs_b = probs_f.astype(jnp.bfloat16)
        value_part = lax.dot_general(
            probs_b, grad_rows, (((0,), (0,)), ((), ())), preferred_element_type=jnp.float32
        )
        grad_probs = lax.dot_general(
            grad_rows, value_tile, (((1,), (1,)), ((), ())), preferred_element_type=jnp.float32
        )
        grad_scores = (probs_f * (grad_probs - row_delta[:, None])).astype(jnp.bfloat16)
        query_grad = query_grad + jnp.dot(grad_scores, key_tile, preferred_element_type=jnp.float32)
        key_part = lax.dot_general(
            grad_scores, query_rows, (((0,), (0,)), ((), ())), preferred_element_type=jnp.float32
        )
        key_acc = lax.dynamic_update_slice_in_dim(
            key_acc,
            lax.dynamic_slice_in_dim(key_acc, tile_start, tile_size, 0) + key_part,
            tile_start,
            0,
        )
        value_acc = lax.dynamic_update_slice_in_dim(
            value_acc,
            lax.dynamic_slice_in_dim(value_acc, tile_start, tile_size, 0) + value_part,
            tile_start,
            0,
        )
        return (query_grad, key_acc, value_acc)

    start_state = (jnp.zeros((row_count, head_size), jnp.float32), key_grad, value_grad)
    return lax.fori_loop(0, tile_limit, tile_step, start_state)


def shards(
    tokens,
    positions,
    qkv_weight,
    out_weight,
    gate_up_weight,
    down_weight,
    norm_gains,
    qk_gains,
    cotangent,
):
    row_count = tokens.shape[1]
    all_places = positions[0]
    length = all_places.shape[0]
    places = lax.dynamic_slice_in_dim(all_places, lax.axis_index("ctx") * row_count, row_count, 0)
    qkv_full, out_full, gate_up_full, down_full = (
        lax.all_gather(qkv_weight, "fsdp", axis=0, tiled=True),
        lax.all_gather(out_weight, "fsdp", axis=0, tiled=True),
        lax.all_gather(gate_up_weight, "fsdp", axis=0, tiled=True),
        lax.all_gather(down_weight, "fsdp", axis=0, tiled=True),
    )
    head_size = qk_gains.shape[1]
    query_width = out_full.shape[0]
    head_count = query_width // head_size
    hidden_size = down_full.shape[0]
    head_scale = head_size ** (-0.5)
    inputs_f = tokens[0].astype(jnp.float32)
    normed_in, inv_in = rms_forward(inputs_f, norm_gains[0])
    normed_in_b = normed_in.astype(jnp.bfloat16)
    projected = jnp.dot(normed_in_b, qkv_full, preferred_element_type=jnp.float32)
    query_pre = projected[:, :query_width].reshape(row_count, head_count, head_size)
    key_pre = projected[:, query_width : query_width + head_size]
    value_b = projected[:, query_width + head_size :].astype(jnp.bfloat16)
    cosine, sine_part = rope_tables(places, head_size)
    query_norm, inv_query = rms_forward(query_pre, qk_gains[0])
    key_norm, inv_key = rms_forward(key_pre, qk_gains[1])
    query_b = (rotate(query_norm, cosine[:, None, :], sine_part[:, None, :]) * head_scale).astype(
        jnp.bfloat16
    )
    key_b = rotate(key_norm, cosine, sine_part).astype(jnp.bfloat16)
    key_whole, value_whole = (
        lax.all_gather(key_b, "ctx", axis=0, tiled=True),
        lax.all_gather(value_b, "ctx", axis=0, tiled=True),
    )
    order_index = (
        jnp.zeros((length,), jnp.int32).at[all_places].set(jnp.arange(length, dtype=jnp.int32))
    )
    key_sorted = key_whole[order_index]
    value_sorted = value_whole[order_index]
    half_rows = row_count // 2
    group_rows = half_rows * head_count
    query_groups = query_b.reshape(2, group_rows, head_size)
    place_groups = jnp.repeat(places, head_count).reshape(2, group_rows)
    mixed_parts = []
    log_parts = []
    for group_index in range(2):
        mixed_part, log_part = attend_forward(
            query_groups[group_index], place_groups[group_index], key_sorted, value_sorted
        )
        mixed_parts.append(mixed_part)
        log_parts.append(log_part)
    mixed_b = jnp.concatenate(mixed_parts, 0).astype(jnp.bfloat16).reshape(row_count, query_width)
    attn_out = jnp.dot(mixed_b, out_full, preferred_element_type=jnp.float32)
    attn_norm, inv_attn = rms_forward(attn_out, norm_gains[1])
    resid = inputs_f + attn_norm
    normed_ff, inv_ff = rms_forward(resid, norm_gains[2])
    normed_ff_b = normed_ff.astype(jnp.bfloat16)
    gate_up = jnp.dot(normed_ff_b, gate_up_full, preferred_element_type=jnp.float32)
    gate_part = gate_up[:, :hidden_size]
    up_part = gate_up[:, hidden_size:]
    activated, gelu_pull = jax.vjp(gelu_tanh, gate_part)
    hidden_b = (activated * up_part).astype(jnp.bfloat16)
    ffn_out = jnp.dot(hidden_b, down_full, preferred_element_type=jnp.float32)
    ffn_norm, inv_out = rms_forward(ffn_out, norm_gains[3])
    output = resid + ffn_norm
    grad_f = cotangent[0].astype(jnp.float32)
    d_ffn, gain_three = rms_backward(ffn_out, inv_out, norm_gains[3], grad_f)
    d_ffn_b = d_ffn.astype(jnp.bfloat16)
    grad_down_full = jnp.dot(hidden_b.T, d_ffn_b, preferred_element_type=jnp.float32)
    d_hidden = jnp.dot(d_ffn_b, down_full.T, preferred_element_type=jnp.float32)
    d_gate = gelu_pull(d_hidden * up_part)[0]
    d_gate_up_b = jnp.concatenate([d_gate, d_hidden * activated], 1).astype(jnp.bfloat16)
    grad_gate_up_full = jnp.dot(normed_ff_b.T, d_gate_up_b, preferred_element_type=jnp.float32)
    d_normed_ff = jnp.dot(d_gate_up_b, gate_up_full.T, preferred_element_type=jnp.float32)
    d_resid_part, gain_two = rms_backward(resid, inv_ff, norm_gains[2], d_normed_ff)
    d_resid = grad_f + d_resid_part
    d_attn, gain_one = rms_backward(attn_out, inv_attn, norm_gains[1], d_resid)
    d_attn_b = d_attn.astype(jnp.bfloat16)
    grad_out_full = jnp.dot(mixed_b.T, d_attn_b, preferred_element_type=jnp.float32)
    d_mixed_b = jnp.dot(d_attn_b, out_full.T, preferred_element_type=jnp.float32).astype(
        jnp.bfloat16
    )
    d_mixed_groups = d_mixed_b.reshape(2, group_rows, head_size)
    mixed_groups = mixed_b.reshape(2, group_rows, head_size)
    delta_groups = jnp.sum(
        d_mixed_groups.astype(jnp.float32) * mixed_groups.astype(jnp.float32), axis=-1
    )
    key_acc = jnp.zeros((length, head_size), jnp.float32)
    value_acc = jnp.zeros((length, head_size), jnp.float32)
    query_parts = []
    for group_index in range(2):
        query_grad, key_acc, value_acc = attend_backward(
            query_groups[group_index],
            place_groups[group_index],
            d_mixed_groups[group_index],
            log_parts[group_index],
            delta_groups[group_index],
            key_sorted,
            value_sorted,
            key_acc,
            value_acc,
        )
        query_parts.append(query_grad)
    d_query = jnp.concatenate(query_parts, 0).reshape(row_count, head_count, head_size)
    key_grad_own, value_grad_own = (
        lax.psum_scatter(key_acc[all_places], "ctx", scatter_dimension=0, tiled=True),
        lax.psum_scatter(value_acc[all_places], "ctx", scatter_dimension=0, tiled=True),
    )
    d_query_norm = rotate(d_query * head_scale, cosine[:, None, :], -sine_part[:, None, :])
    d_query_pre, gain_query = rms_backward(query_pre, inv_query, qk_gains[0], d_query_norm)
    d_key_norm = rotate(key_grad_own, cosine, -sine_part)
    d_key_pre, gain_key = rms_backward(key_pre, inv_key, qk_gains[1], d_key_norm)
    d_projected_b = jnp.concatenate(
        [d_query_pre.reshape(row_count, query_width), d_key_pre, value_grad_own], 1
    ).astype(jnp.bfloat16)
    grad_qkv_full = jnp.dot(normed_in_b.T, d_projected_b, preferred_element_type=jnp.float32)
    d_normed_in = jnp.dot(d_projected_b, qkv_full.T, preferred_element_type=jnp.float32)
    d_inputs, gain_zero = rms_backward(inputs_f, inv_in, norm_gains[0], d_normed_in)
    grad_tokens = d_resid + d_inputs
    grad_qkv_part, grad_out_part, grad_gate_up_part, grad_down_part = (
        lax.psum_scatter(
            grad_qkv_full.astype(jnp.bfloat16), "fsdp", scatter_dimension=0, tiled=True
        ).astype(jnp.float32),
        lax.psum_scatter(
            grad_out_full.astype(jnp.bfloat16), "fsdp", scatter_dimension=0, tiled=True
        ).astype(jnp.float32),
        lax.psum_scatter(
            grad_gate_up_full.astype(jnp.bfloat16), "fsdp", scatter_dimension=0, tiled=True
        ).astype(jnp.float32),
        lax.psum_scatter(
            grad_down_full.astype(jnp.bfloat16), "fsdp", scatter_dimension=0, tiled=True
        ).astype(jnp.float32),
    )
    gains_local = jnp.stack([gain_zero, gain_one, gain_two, gain_three], 0)
    qk_local = jnp.stack([gain_query, gain_key], 0)
    summed = lax.psum(
        (grad_qkv_part, grad_out_part, grad_gate_up_part, grad_down_part, gains_local, qk_local),
        "ctx",
    )
    gains_total, qk_total = lax.psum((summed[4], summed[5]), "fsdp")
    return (
        output[None],
        grad_tokens[None],
        summed[0],
        summed[1],
        summed[2],
        summed[3],
        gains_total,
        qk_total,
    )


def solution(mesh):
    in_specs = (
        P("fsdp", "ctx", None),
        P("fsdp", None),
        P("fsdp", None),
        P("fsdp", None),
        P("fsdp", None),
        P("fsdp", None),
        P(),
        P(),
        P("fsdp", "ctx", None),
    )
    out_specs = (
        P("fsdp", "ctx", None),
        P("fsdp", "ctx", None),
        P("fsdp", None),
        P("fsdp", None),
        P("fsdp", None),
        P("fsdp", None),
        P(),
        P(),
    )
    return jax.shard_map(shards, mesh=mesh, in_specs=in_specs, out_specs=out_specs, check_vma=False)
```

profile of v0, /device:TPU:0, one launch (start us, length us, event | category | flops | bytes accessed | tf_op | source)
XLA Modules:
  0.0 680.4 jit_solution(233254995933849721)
XLA Ops:
  7.3 0.7 all-gather.5.cloned.1.call-update
  8.0 0.7 all-gather.7.cloned.1.call-update
  8.7 0.7 all-gather.9.cloned.1.call-update
  16.9 4.3 scatter_custom_fusion
  21.5 12.6 %all-gather.5.cloned.1.call-done = bf16[640,1536]{1,0:T(8,128)(2,1)} async-done(((bf16[160,1536]{1,0:T(8,128)(2,1)}), bf16[640,1536]{1,0:T(8,128)(2,1)}) %all-gather.5.cloned.1.call-update) | async-done | bytes 1966096 | tf_op jit(solution)/shard_map/all_gather | solution.py:158
  34.2 2.1 fusion.118
  37.1 31.4 %all_gather.19 = bf16[1024,256]{1,0:T(8,128)(2,1)S(1)} all-gather(bf16[128,256]{1,0:T(8,128)(2,1)S(1)} %get-tuple-element.608), channel_id=1, replica_groups=mesh['ctx'=8,'fsdp'=4] {'ctx'}, dimensions={0}, use_global_device_ids=true | all-gather | bytes 589824 | tf_op jit(solution)/shard_map/all_gather | solution.py:183
  70.0 3.9 gather_fusion
  74.6 31.5 %all_gather.20 = bf16[1024,256]{1,0:T(8,128)(2,1)S(1)} all-gather(bf16[128,256]{1,0:T(8,128)(2,1)S(1)} %slice.229), channel_id=1, replica_groups=mesh['ctx'=8,'fsdp'=4] {'ctx'}, dimensions={0}, use_global_device_ids=true | all-gather | bytes 589824 | tf_op jit(solution)/shard_map/all_gather | solution.py:184
  106.1 3.9 gather_fusion.1
  110.1 1.4 while.78
  111.5 0.8 while.81
  112.8 1.8 while.79
  115.2 1.9 multiply_reduce_fusion.9
  117.3 3.6 fusion.128
  121.0 1.3 copy-done.10
  123.0 2.6 multiply_reduce_fusion.7
  125.6 0.7 fusion.111
  126.3 0.9 fusion.102
  127.3 1.4 fusion.88
  129.2 2.4 multiply_reduce_fusion.3
  131.6 0.8 multiply_reduce_fusion.4
  132.4 0.7 copy-done.19
  133.9 0.7 fusion.132
  135.5 0.8 broadcast.294.clone.2
  136.4 11.3 %while.82 = (s32[]{:T(128)}, f32[256,256]{1,0:T(8,128)}, f32[1024,256]{1,0:T(8,128)S(1)}, f32[1024,256]{1,0:T(8,128)S(1)}, s32[]{:T(128)}, /*index=5*/bf16[1024,...) while((s32[]{:T(128)}, f32[256,256]{1,0:T(8,128)}, ...), condition=%wide.region_26.27_spmd.clone, body=%wide.region_25.26_spmd.clone.sunk | while | flops 336790016 | bytes 8399387 | solution.py:139
  136.4 0.7 broadcast_in_dim.145
  137.1 1.4 le.181
  139.1 1.0 fusion.229
  140.1 0.9 fusion.230
  142.0 0.7 broadcast_in_dim.145
  142.7 1.4 le.181
  144.7 1.0 fusion.229
  145.7 0.9 fusion.230
  147.7 1.0 squeeze.14
  148.7 0.7 broadcast.294
  149.4 3.1 while.83
  149.6 0.9 fusion.243
  150.6 0.9 fusion.244
  152.5 4.7 gather_fusion.2
  157.3 4.7 gather_fusion.3
  162.0 1.6 convolution_convert_fusion.3
  163.7 2.4 convolution_convert_fusion.2
  168.3 52.4 %reduce-scatter.7.cloned.1.call-done = f32[128,256]{1,0:T(8,128)} async-done(((f32[1024,256]{1,0:T(8,128)}), f32[128,256]{1,0:T(8,128)}) %reduce-scatter.7.cloned.1.call-update) | async-done | bytes 131088 | tf_op jit(solution)/shard_map/reduce_scatter | solution.py:257
  220.7 0.9 slice_negate_fusion.2
  221.6 2.2 multiply_reduce_fusion.10
  223.9 1.1 multiply_reduce_fusion
  225.5 0.9 copy.18
  226.4 60.5 %reduce-scatter.9.cloned.1.call-done = f32[128,256]{1,0:T(8,128)} async-done(((f32[1024,256]{1,0:T(8,128)}), f32[128,256]{1,0:T(8,128)}) %reduce-scatter.9.cloned.1.call-update) | async-done | bytes 131088 | tf_op jit(solution)/shard_map/reduce_scatter | solution.py:258
  286.9 0.9 convert.27
  288.4 0.7 multiply_convert_fusion.5
  289.2 1.4 multiply_convert_fusion.2
  290.6 0.7 copy-done.30
  291.3 2.1 convolution_convert_fusion.1
  293.5 4.0 convolution_convert_fusion
  298.2 0.9 copy-done.24
  299.1 0.8 fusion.109
  300.0 0.9 fusion.108
  300.9 14.7 %reduce-scatter.13.cloned.1.call-done = bf16[256,640]{1,0:T(8,128)(2,1)} async-done(((bf16[1024,640]{1,0:T(8,128)(2,1)}), bf16[256,640]{1,0:T(8,128)(2,1)}) %reduce-scatter.13.cloned.1.call-update) | async-done | bytes 327696 | tf_op jit(solution)/shard_map/reduce_scatter | solution.py:275
  315.6 38.0 %reduce-scatter.17.cloned.1.call-done = bf16[512,640]{1,0:T(8,128)(2,1)} async-done(((bf16[2048,640]{1,0:T(8,128)(2,1)}), bf16[512,640]{1,0:T(8,128)(2,1)}) %reduce-scatter.17.cloned.1.call-update) | async-done | bytes 655376 | tf_op jit(solution)/shard_map/reduce_scatter | solution.py:281
  353.5 33.3 %reduce-scatter.11.cloned.1.call-done = bf16[160,1536]{1,0:T(8,128)(2,1)} async-done(((bf16[640,1536]{1,0:T(8,128)(2,1)}), bf16[160,1536]{1,0:T(8,128)(2,1)}) %reduce-scatter.11.cloned.1.call-update) | async-done | bytes 491536 | tf_op jit(solution)/shard_map/reduce_scatter | solution.py:272
  386.8 53.9 %reduce-scatter.15.cloned.1.call-done = bf16[160,4096]{1,0:T(8,128)(2,1)} async-done(((bf16[640,4096]{1,0:T(8,128)(2,1)}), bf16[160,4096]{1,0:T(8,128)(2,1)}) %reduce-scatter.15.cloned.1.call-update) | async-done | bytes 1310736 | tf_op jit(solution)/shard_map/reduce_scatter | solution.py:278
  440.8 222.0 %all-reduce.3 = (f32[160,1536]{1,0:T(8,128)}, f32[256,640]{1,0:T(8,128)}, f32[160,4096]{1,0:T(8,128)}, f32[512,640]{1,0:T(8,128)}, f32[4,640]{1,0:T(4,128)S(1)}, /*index=5*/f32[2,256]{1,0:T(2,128)S(1)}) all-reduce(bf16[160,1536]{1,0:T(8,128)(2,1)} %reduce-scatter.11.cloned.1.call-done, ...), channel_id=1, replica_groups=mesh['ctx'=8,'fsdp'=4] {'ctx'}, use_global_device_ids=true, to_apply=%region_35.36 | all-reduce | flops 1395712 | bytes 8380416 | tf_op jit(solution)/shard_map/psum | solution.py:287
  662.7 10.8 %all-reduce.1 = (f32[4,640]{1,0:T(4,128)}, f32[2,256]{1,0:T(2,128)}) all-reduce(f32[4,640]{1,0:T(4,128)S(1)} %get-tuple-element.574, f32[2,256]{1,0:T(2,128)S(1)} %get-tuple-element.575), channel_id=1, replica_groups=mesh['ctx'=8,'fsdp'=4] {'fsdp'}, use_global_device_ids=true, to_apply=%region_47.48 | all-reduce | flops 3072 | bytes 24576 | tf_op jit(solution)/shard_map/psum | solution.py:291
  (290 shorter events, 22.5 us)
Async XLA Ops:
  7.2 2.9 copy-start.58
  7.2 8.8 %copy-start.56 = (f32[4,640]{1,0:T(4,128)S(1)}, f32[4,640]{1,0:T(4,128)}, u32[]{:S(2)}) copy-start(f32[4,640]{1,0:T(4,128)} %param.27) | copy-start | bytes 30724
  7.2 8.9 %copy-start.17 = (bf16[1,128,640]{2,1,0:T(8,128)(2,1)S(1)}, bf16[1,128,640]{2,1,0:T(8,128)(2,1)}, u32[]{:S(2)}) copy-start(bf16[1,128,640]{2,1,0:T(8,128)(2,1)} %param.21) | copy-start | bytes 491524
  7.2 9.0 %copy-start.65 = (f32[2,256]{1,0:T(2,128)S(1)}, f32[2,256]{1,0:T(2,128)}, u32[]{:S(2)}) copy-start(f32[2,256]{1,0:T(2,128)} %param.28) | copy-start | bytes 6148
  7.2 27.0 %all-gather.5.cloned.1.call-start = ((), (), s32[]{:S(2)}) async-start(), calls=%async_computation.6 | async-start | bytes 2457600 | tf_op jit(solution)/shard_map/all_gather | solution.py:158
  7.9 107.2 %all-gather.7.cloned.1.call-start = ((), (), s32[]{:S(2)}) async-start(), calls=%async_computation.7 | async-start | bytes 1638400 | tf_op jit(solution)/shard_map/all_gather | solution.py:159
  8.7 108.6 %all-gather.9.cloned.1.call-start = ((), (), s32[]{:S(2)}) async-start(), calls=%async_computation.8 | async-start | bytes 6553600 | tf_op jit(solution)/shard_map/all_gather | solution.py:160
  9.4 113.6 %all-gather.11.cloned.1.call-start = ((), (), s32[]{:S(2)}) async-start(), calls=%async_computation.9 | async-start | bytes 3276800 | tf_op jit(solution)/shard_map/all_gather | solution.py:161
  10.0 210.7 %reduce-scatter.7.cloned.1.call-start = ((), (), s32[]{:S(2)}) async-start(), calls=%async_computation.10 | async-start | bytes 1179648 | tf_op jit(solution)/shard_map/reduce_scatter | solution.py:257
  16.2 20.2 %copy-start.59 = (f32[128]{0:T(128)}, f32[128]{0:T(128)S(1)}, u32[]{:S(2)}) copy-start(f32[128]{0:T(128)S(1)} %add_rsqrt_fusion.5) | copy-start | bytes 1540
  16.3 20.3 %copy-start.47 = (f32[1,256]{1,0:T(1,128)}, f32[1,256]{1,0:T(1,128)S(1)}, u32[]{:S(2)}) copy-start(f32[1,256]{1,0:T(1,128)S(1)} %get-tuple-element.613) | copy-start | bytes 3076
  16.3 53.2 %copy-start.49 = (f32[1,256]{1,0:T(1,128)}, f32[1,256]{1,0:T(1,128)S(1)}, u32[]{:S(2)}) copy-start(f32[1,256]{1,0:T(1,128)S(1)} %get-tuple-element.612) | copy-start | bytes 3076
  21.5 15.1 %copy-start.34 = (f32[128,128]{1,0:T(8,128)}, f32[128,128]{1,0:T(8,128)S(1)}, u32[]{:S(2)}) copy-start(f32[128,128]{1,0:T(8,128)S(1)} %get-tuple-element.614) | copy-start | bytes 196612
  21.5 15.1 %copy-start.36 = (f32[128,128]{1,0:T(8,128)}, f32[128,128]{1,0:T(8,128)S(1)}, u32[]{:S(2)}) copy-start(f32[128,128]{1,0:T(8,128)S(1)} %get-tuple-element.615) | copy-start | bytes 196612
  36.5 32.8 %copy-start.57 = (f32[128]{0:T(128)}, f32[128]{0:T(128)S(1)}, u32[]{:S(2)}) copy-start(f32[128]{0:T(128)S(1)} %add_rsqrt_fusion.4) | copy-start | bytes 1540
  115.2 1.9 copy-start.22
  117.3 14.3 %copy-start.8 = (f32[128,640]{1,0:T(8,128)}, f32[128,640]{1,0:T(8,128)S(1)}, u32[]{:S(2)}) copy-start(f32[128,640]{1,0:T(8,128)S(1)} %get-tuple-element.582) | copy-start | bytes 983044
  117.3 14.3 %copy-start.54 = (f32[128]{0:T(128)}, f32[128]{0:T(128)S(1)}, u32[]{:S(2)}) copy-start(f32[128]{0:T(128)S(1)} %add_rsqrt_fusion.2) | copy-start | bytes 1540
  122.7 4.6 copy-start.15
  122.7 2.9 copy-start.27
  123.0 4.2 copy-start.11
  123.0 4.2 copy-start.21
  126.3 2.4 slice-start
  127.2 1.9 slice-start.1
  128.6 2.9 copy-start.37
  128.7 2.9 copy-start.39
  131.6 1.7 copy-start.14
  133.3 3.0 copy-start.28
  139.1 1.9 copy-start.5
  144.7 1.9 copy-start.5
  149.4 3.1 copy-start.46
  149.6 1.9 copy-start.2
  157.2 129.7 %reduce-scatter.9.cloned.1.call-start = ((), (), s32[]{:S(2)}) async-start(), calls=%async_computation.11 | async-start | bytes 1179648 | tf_op jit(solution)/shard_map/reduce_scatter | solution.py:258
  157.2 4.8 copy-start.23
  157.3 4.8 copy-start.29
  161.9 1.8 copy-start.16
  161.9 1.8 copy-start.33
  162.0 153.6 %reduce-scatter.13.cloned.1.call-start = ((), (), s32[]{:S(2)}) async-start(), calls=%async_computation.13 | async-start | bytes 1638400 | tf_op jit(solution)/shard_map/reduce_scatter | solution.py:275
  163.7 189.9 %reduce-scatter.17.cloned.1.call-start = ((), (), s32[]{:S(2)}) async-start(), calls=%async_computation.15 | async-start | bytes 3276800 | tf_op jit(solution)/shard_map/reduce_scatter | solution.py:281
  166.1 1.6 copy-start.7
  166.1 1.6 copy-start.4
  166.1 220.7 %reduce-scatter.11.cloned.1.call-start = ((), (), s32[]{:S(2)}) async-start(), calls=%async_computation.12 | async-start | bytes 2457600 | tf_op jit(solution)/shard_map/reduce_scatter | solution.py:272
  167.7 53.9 %copy-start.13 = (f32[128,1536]{1,0:T(8,128)S(1)}, f32[128,1536]{1,0:T(8,128)}, u32[]{:S(2)}) copy-start(f32[128,1536]{1,0:T(8,128)} %copy-done.12) | copy-start | bytes 2359300
  167.8 53.9 %copy-start.35 = (f32[128,128]{1,0:T(8,128)S(1)}, f32[128,128]{1,0:T(8,128)}, u32[]{:S(2)}) copy-start(f32[128,128]{1,0:T(8,128)} %copy-done.34) | copy-start | bytes 196612
  167.8 53.9 %copy-start.48 = (f32[1,256]{1,0:T(1,128)S(1)}, f32[1,256]{1,0:T(1,128)}, u32[]{:S(2)}) copy-start(f32[1,256]{1,0:T(1,128)} %copy-done.47) | copy-start | bytes 3076
  167.9 55.9 %copy-start.1 = (f32[128,4,256]{2,1,0:T(4,128)S(1)}, f32[128,4,256]{2,1,0:T(4,128)}, u32[]{:S(2)}) copy-start(f32[128,4,256]{2,1,0:T(4,128)} %copy-done) | copy-start | bytes 1572868
  225.2 63.3 %copy-start.41 = (f32[128,256]{1,0:T(8,128)S(1)}, f32[128,256]{1,0:T(8,128)}, u32[]{:S(2)}) copy-start(f32[128,256]{1,0:T(8,128)} %get-tuple-element.579) | copy-start | bytes 393220
  225.2 64.0 %copy-start.51 = (f32[1,2,4,128]{3,1,2,0:T(2,128)S(1)}, f32[1,2,4,128]{3,1,2,0:T(2,128)}, u32[]{:S(2)}) copy-start(f32[1,2,4,128]{3,1,2,0:T(2,128)} %copy.20) | copy-start | bytes 12292
  226.4 64.9 %copy-start.18 = (bf16[1,128,640]{2,1,0:T(8,128)(2,1)S(1)}, bf16[1,128,640]{2,1,0:T(8,128)(2,1)}, u32[]{:S(2)}) copy-start(bf16[1,128,640]{2,1,0:T(8,128)(2,1)} %param.21) | copy-start | bytes 491524
  226.4 64.9 %copy-start.60 = (f32[128]{0:T(128)S(1)}, f32[128]{0:T(128)}, u32[]{:S(2)}) copy-start(f32[128]{0:T(128)} %copy-done.59) | copy-start | bytes 1540
  287.8 2.8 copy-start.42
  291.3 2.2 copy-start.9
  291.3 2.2 copy-start.38
  291.3 2.2 copy-start.40
  291.3 2.2 copy-start.55
  293.4 147.4 %reduce-scatter.15.cloned.1.call-start = ((), (), s32[]{:S(2)}) async-start(), calls=%async_computation.14 | async-start | bytes 6553600 | tf_op jit(solution)/shard_map/reduce_scatter | solution.py:278
  297.5 1.6 copy-start.24
  297.5 1.6 copy-start.31
  297.5 1.6 copy-start.43
  297.5 1.6 copy-start.45
  297.5 1.6 copy-start.61
  297.5 2.4 copy-start.62
  297.6 2.4 copy-start.64
  297.6 2.4 copy-start.20
  (18 other events, 15.6 us)
Sparse Core Ops, SparseCore 0:
  9.6 24.5 all-gather.4
  35.7 18.1 all-gather.6
  55.5 40.4 all-gather.8
  97.4 25.5 all-gather.10
  157.3 63.3 reduce-scatter.6
  224.4 62.4 reduce-scatter.8
  290.0 25.5 reduce-scatter.12
  318.8 34.6 reduce-scatter.16
  356.1 30.6 reduce-scatter.10
  389.4 51.3 reduce-scatter.14
where the time goes:
time: 681 us; the launch traced here: 680 us
  blocking collectives  296 us (43%)
  waiting for transfers between devices  268 us (39%)
  local copies, waits for them, and re-layouts  41.8 us (6%)
  matrix products  35.7 us (5%)
  between operations  20.6 us (3%)
  other arithmetic  16.9 us (2%)
    psum x1, blocking collectives, shards(): lax.psum((grad_qkv_part, grad_out_part, grad_gate_up_part, grad_down_part...  222 us
    reduce_scatter x1, waiting for transfers between devices, shards(): lax.psum_scatter(value_acc[all_places], 'ctx', scatter_dimension=0, tiled...  60.5 us
    reduce_scatter x1, waiting for transfers between devices, shards(): lax.psum_scatter(grad_gate_up_full.astype(jnp.bfloat16), 'fsdp', scatter_...  53.9 us
    reduce_scatter x1, waiting for transfers between devices, shards(): lax.psum_scatter(key_acc[all_places], 'ctx', scatter_dimension=0, tiled=T...  52.4 us
    reduce_scatter x1, waiting for transfers between devices, shards(): lax.psum_scatter(grad_down_full.astype(jnp.bfloat16), 'fsdp', scatter_dim...  38 us
    reduce_scatter x1, waiting for transfers between devices, shards(): lax.psum_scatter(grad_qkv_full.astype(jnp.bfloat16), 'fsdp', scatter_dime...  33.3 us
    all_gather x1, blocking collectives, shards(): lax.all_gather(value_b, 'ctx', axis=0, tiled=True)  31.5 us
    all_gather x1, blocking collectives, shards(): lax.all_gather(key_b, 'ctx', axis=0, tiled=True)  31.4 us
  transfers between devices with their start and end apart: 10, of which 8 were waited for; matrix products, arithmetic and copies ran while one was open for 8% of the time, Pallas kernels for 0%

commit v1 on v0

v1 whole, which is shorter than its diff:
```python
import functools

import jax
import jax.numpy as jnp
from jax import lax
from jax.experimental import pallas as pl
from jax.experimental.pallas import tpu as pltpu
from jax.sharding import PartitionSpec as P

EPS = 1e-06
ROPE_BASE = 1000000.0
NEG = -1e30
BF = jnp.bfloat16
F32 = jnp.float32
MESH = pl.DeviceIdType.MESH
VMEM_LIMIT = 60 * 1024 * 1024


def rms_forward(entries, weight):
    inv_rms = lax.rsqrt(jnp.mean(entries * entries, axis=-1, keepdims=True) + EPS)
    return (entries * inv_rms * (1.0 + weight), inv_rms)


def rms_backward(entries, inv_rms, weight, incoming):
    normed = entries * inv_rms
    scaled = incoming * (1.0 + weight)
    lead_axes = tuple(range(incoming.ndim - 1))
    d_weight = jnp.sum(incoming * normed, axis=lead_axes)
    d_entries = inv_rms * (scaled - normed * jnp.mean(scaled * normed, axis=-1, keepdims=True))
    return (d_entries, d_weight)


def rope_tables(places, head_size):
    half_size = head_size // 2
    frequency = ROPE_BASE ** (-2.0 * jnp.arange(half_size, dtype=jnp.float32) / head_size)
    angles = places.astype(jnp.float32)[:, None] * frequency[None, :]
    cosine = jnp.cos(angles)
    sine_part = jnp.sin(angles)
    return (jnp.concatenate([cosine, cosine], -1), jnp.concatenate([sine_part, sine_part], -1))


def rotate(entries, cosine, sine_part):
    half_size = entries.shape[-1] // 2
    turned = jnp.concatenate([-entries[..., half_size:], entries[..., :half_size]], -1)
    return entries * cosine + turned * sine_part


def gelu_tanh(entries):
    return jax.nn.gelu(entries, approximate=True)


def nt(left, right):
    return lax.dot_general(left, right, (((1,), (1,)), ((), ())), preferred_element_type=F32)


def tn(left, right):
    return lax.dot_general(left, right, (((0,), (0,)), ((), ())), preferred_element_type=F32)


def nn(left, right):
    return jnp.dot(left, right, preferred_element_type=F32)


class Place:
    def __init__(self, zn):
        ctx, fsdp = lax.axis_index("ctx"), lax.axis_index("fsdp")
        self.zn = zn
        self.z, self.y = ctx // 2, lax.rem(ctx, 2)
        self.x, self.c = fsdp // 2, lax.rem(fsdp, 2)
        self.ctx, self.fsdp = ctx, fsdp
        self.core_peer = (ctx, self.x * 2 + 1 - self.c)
        self.x_peer = (ctx, (1 - self.x) * 2 + self.c)
        self.y_peer = (self.z * 2 + 1 - self.y, fsdp)

    def z_index(self, step):
        return lax.rem(self.z + step, self.zn)

    def z_peer(self, step):
        return (self.z_index(step) * 2 + self.y, self.fsdp)


def greet(peers):
    barrier = pltpu.get_barrier_semaphore()
    for peer in peers:
        pl.semaphore_signal(barrier, inc=1, device_id=peer, device_id_type=MESH)
    pl.semaphore_wait(barrier, len(peers))


class Sender:
    def __init__(self, send_sem, recv_sem):
        self.send_sem, self.recv_sem = send_sem, recv_sem
        self.used = 0
        self.copies = []

    def start(self, source, target, peer):
        slot = self.used
        self.used += 1
        copy = pltpu.make_async_remote_copy(
            src_ref=source,
            dst_ref=target,
            send_sem=self.send_sem.at[slot],
            recv_sem=self.recv_sem.at[slot],
            device_id=peer,
            device_id_type=MESH,
        )
        copy.start()
        self.copies.append(copy)
        return copy

    def finish(self):
        for copy in self.copies:
            copy.wait_send()


def rows_at(start, size):
    return pl.ds(pl.multiple_of(start, 16), size)


def gather_kernel(plan, count, zn, *refs):
    ins, outs = refs[:count], refs[count : 2 * count]
    send_sem, recv_sem, own_sem = refs[2 * count :]
    here = Place(zn)
    greet([here.core_peer, here.x_peer, here.y_peer])
    sender = Sender(send_sem, recv_sem)
    own_copies = []
    state = {}

    def spot(chunk, quarter, half):
        index, col, width = chunk
        rows = ins[index].shape[0]
        if half is None:
            return outs[index].at[rows_at(quarter * rows, rows), pl.ds(col, width)]
        return outs[index].at[
            rows_at(quarter * rows + half * (rows // 2), rows // 2), pl.ds(col, width)
        ]

    def stage(level, at):
        chunk = plan[at]
        index, col, width = chunk
        rows = ins[index].shape[0]
        far = (1 - here.x) * 2 + here.c
        if level == 0:
            half = ins[index].at[rows_at(here.y * (rows // 2), rows // 2), pl.ds(col, width)]
            whole = ins[index].at[:, pl.ds(col, width)]
            to_x = sender.start(half, spot(chunk, here.fsdp, here.y), here.x_peer)
            to_core = sender.start(whole, spot(chunk, here.fsdp, None), here.core_peer)
            own = pltpu.make_async_copy(whole, spot(chunk, here.fsdp, None), own_sem.at[at])
            own.start()
            own_copies.append(own)
            state[at] = [to_x, to_core]
        elif level == 1:
            state[at][0].wait_recv()
            block = spot(chunk, far, here.y)
            state[at].append(sender.start(block, block, here.y_peer))
            state[at].append(sender.start(block, block, here.core_peer))
        elif level == 2:
            state[at][2].wait_recv()
            block = spot(chunk, far, 1 - here.y)
            state[at].append(sender.start(block, block, here.core_peer))
        else:
            for part in (1, 3, 4):
                state[at][part].wait_recv()

    for at in range(len(plan)):
        stage(0, at)
    for tick in range(len(plan) + 2):
        for level in (3, 2, 1):
            at = tick - (level - 1)
            if 0 <= at < len(plan):
                stage(level, at)
    for own in own_copies:
        own.wait()
    sender.finish()


def gather_weights(arrays, zn):
    plan = []
    for index, array in enumerate(arrays):
        width = array.shape[1]
        step = width if width <= 1536 else 1024
        plan += [(index, col, step) for col in range(0, width, step)]
    count = len(arrays)
    return pl.pallas_call(
        functools.partial(gather_kernel, plan, count, zn),
        out_shape=[
            jax.ShapeDtypeStruct((4 * array.shape[0], array.shape[1]), array.dtype)
            for array in arrays
        ],
        in_specs=[pl.BlockSpec(memory_space=pltpu.VMEM)] * count,
        out_specs=[pl.BlockSpec(memory_space=pltpu.VMEM)] * count,
        scratch_shapes=[
            pltpu.SemaphoreType.DMA((5 * len(plan),)),
            pltpu.SemaphoreType.DMA((5 * len(plan),)),
            pltpu.SemaphoreType.DMA((len(plan),)),
        ],
        compiler_params=pltpu.CompilerParams(
            collective_id=0, has_side_effects=True, vmem_limit_bytes=VMEM_LIMIT
        ),
    )(*arrays)


def kv_gather_kernel(zn, in_ref, out_ref, send_sem, recv_sem, own_sem):
    here = Place(zn)
    greet([here.y_peer] + [here.z_peer(step) for step in range(1, zn)])
    sender = Sender(send_sem, recv_sem)
    along_z = [
        sender.start(in_ref, out_ref.at[here.ctx], here.z_peer(step)) for step in range(1, zn)
    ]
    along_y = [sender.start(in_ref, out_ref.at[here.ctx], here.y_peer)]
    own = pltpu.make_async_copy(in_ref, out_ref.at[here.ctx], own_sem.at[0])
    own.start()
    for step in range(1, zn):
        along_z[step - 1].wait_recv()
        block = out_ref.at[here.z_index(zn - step) * 2 + here.y]
        along_y.append(sender.start(block, block, here.y_peer))
    for copy in along_y:
        copy.wait_recv()
    own.wait()
    sender.finish()


def gather_kv(block, zn):
    return pl.pallas_call(
        functools.partial(kv_gather_kernel, zn),
        out_shape=jax.ShapeDtypeStruct((2 * zn,) + block.shape, block.dtype),
        in_specs=[pl.BlockSpec(memory_space=pltpu.VMEM)],
        out_specs=pl.BlockSpec(memory_space=pltpu.VMEM),
        scratch_shapes=[
            pltpu.SemaphoreType.DMA((2 * zn - 1,)),
            pltpu.SemaphoreType.DMA((2 * zn - 1,)),
            pltpu.SemaphoreType.DMA((1,)),
        ],
        compiler_params=pltpu.CompilerParams(
            collective_id=1, has_side_effects=True, vmem_limit_bytes=VMEM_LIMIT
        ),
    )(block)


def kv_reduce_kernel(zn, in_ref, out_ref, from_y, summed, from_z, send_sem, recv_sem):
    here = Place(zn)
    greet([here.y_peer] + [here.z_peer(step) for step in range(1, zn)])
    sender = Sender(send_sem, recv_sem)
    order = list(range(1, zn)) + [0]
    along_y = []
    for step in order:
        target = here.z_index(step)
        along_y.append(
            sender.start(in_ref.at[target * 2 + 1 - here.y], from_y.at[target], here.y_peer)
        )
    along_z = []
    for at, step in enumerate(order):
        along_y[at].wait_recv()
        target = here.z_index(step)
        both = in_ref[target * 2 + here.y].astype(F32) + from_y[target].astype(F32)
        if step == 0:
            out_ref[...] = both
        else:
            summed[step - 1] = both.astype(BF)
            along_z.append(
                sender.start(summed.at[step - 1], from_z.at[step - 1], here.z_peer(step))
            )
    for step in range(1, zn):
        along_z[step - 1].wait_recv()
        out_ref[...] += from_z[step - 1].astype(F32)
    sender.finish()


def reduce_kv(blocks, zn):
    shape = blocks.shape[1:]
    return pl.pallas_call(
        functools.partial(kv_reduce_kernel, zn),
        out_shape=jax.ShapeDtypeStruct(shape, F32),
        in_specs=[pl.BlockSpec(memory_space=pltpu.VMEM)],
        out_specs=pl.BlockSpec(memory_space=pltpu.VMEM),
        scratch_shapes=[
            pltpu.VMEM((zn,) + shape, BF),
            pltpu.VMEM((zn - 1,) + shape, BF),
            pltpu.VMEM((zn - 1,) + shape, BF),
            pltpu.SemaphoreType.DMA((2 * zn - 1,)),
            pltpu.SemaphoreType.DMA((2 * zn - 1,)),
        ],
        compiler_params=pltpu.CompilerParams(
            collective_id=2, has_side_effects=True, vmem_limit_bytes=VMEM_LIMIT
        ),
    )(blocks)


PER_CHUNK = 11


def reduce_kernel(plan, count, zn, *refs):
    ins, small_in = refs[:count], refs[count]
    outs, small_out = refs[count + 1 : 2 * count + 1], refs[2 * count + 1]
    rest = refs[2 * count + 2 :]
    buffers = [rest[5 * at : 5 * at + 5] for at in range(len(plan))]
    small_recv, small_sum, small_z, send_sem, recv_sem = rest[5 * len(plan) :]
    here = Place(zn)
    greet(
        [here.core_peer, here.x_peer, here.y_peer] + [here.z_peer(step) for step in range(1, zn)]
    )
    sender = Sender(send_sem, recv_sem)
    state = {}
    own = here.fsdp
    away = (1 - here.x) * 2 + here.c

    def piece(chunk, z_at):
        index, row, rows, col, width, by_rows = chunk
        half = rows // 2
        if by_rows:
            return (z_at * (half // zn), half // zn, 0, width)
        return (0, half, z_at * (width // zn), width // zn)

    def cut(ref, chunk, z_at, row_base, col_base):
        r0, rows, c0, width = piece(chunk, z_at)
        return ref.at[
            rows_at(row_base + r0, rows), pl.ds(pl.multiple_of(col_base + c0, 128), width)
        ]

    def block(ref, chunk, quarter):
        index, row, rows, col, width, by_rows = chunk
        whole = ref.shape[0] // 4
        return ref.at[rows_at(quarter * whole + row, rows), pl.ds(col, width)]

    def stage(level, at):
        chunk = plan[at]
        index, row, rows, col, width, by_rows = chunk
        from_core, from_x, total, from_y, from_z = buffers[at]
        half = rows // 2
        mine = rows_at(here.y * half, half)
        other = rows_at((1 - here.y) * half, half)
        if level == 0:
            order = (1 - here.x, here.x)
            state[at] = [
                sender.start(
                    block(ins[index], chunk, side * 2 + 1 - here.c),
                    from_core.at[side],
                    here.core_peer,
                )
                for side in (0, 1)
            ]
        elif level == 1:
            for copy in state[at]:
                copy.wait_recv()
            side = 1 - here.x
            from_core[side] = (
                block(ins[index], chunk, away)[...].astype(F32) + from_core[side].astype(F32)
            ).astype(BF)
            state[at] = [sender.start(from_core.at[side], from_x, here.x_peer)]
        elif level == 2:
            state[at][0].wait_recv()
            total[...] = (
                block(ins[index], chunk, own)[...].astype(F32)
                + from_core[here.x].astype(F32)
                + from_x[...].astype(F32)
            ).astype(BF)
            state[at] = [sender.start(total.at[other], from_y, here.y_peer)]
        elif level == 3:
            state[at][0].wait_recv()
            total[mine] = (total[mine].astype(F32) + from_y[...].astype(F32)).astype(BF)
            state[at] = [
                sender.start(
                    cut(total, chunk, here.z_index(step), here.y * half, 0),
                    from_z.at[step - 1],
                    here.z_peer(step),
                )
                for step in range(1, zn)
            ]
        elif level == 4:
            for copy in state[at]:
                copy.wait_recv()
            result = cut(total, chunk, here.z, here.y * half, 0)[...].astype(F32)
            for step in range(1, zn):
                result = result + from_z[step - 1].astype(F32)
            place = cut(outs[index], chunk, here.z, row + here.y * half, col)
            place[...] = result.astype(BF)
            state[at] = [sender.start(place, place, here.z_peer(step)) for step in range(1, zn)]
        elif level == 5:
            for copy in state[at]:
                copy.wait_recv()
            place = outs[index].at[rows_at(row + here.y * half, half), pl.ds(col, width)]
            state[at] = [sender.start(place, place, here.y_peer)]
        else:
            state[at][0].wait_recv()

    def small_stage(level):
        if level == 0:
            state["s"] = [sender.start(small_in, small_recv.at[0], here.core_peer)]
        elif level in (1, 2):
            state["s"][0].wait_recv()
            base = small_in if level == 1 else small_sum.at[0]
            small_sum[level - 1] = base[...] + small_recv[level - 1]
            peer = here.x_peer if level == 1 else here.y_peer
            state["s"] = [sender.start(small_sum.at[level - 1], small_recv.at[level], peer)]
        elif level == 3:
            state["s"][0].wait_recv()
            small_z[here.z] = small_sum[1] + small_recv[2]
            state["s"] = [
                sender.start(small_z.at[here.z], small_z.at[here.z], here.z_peer(step))
                for step in range(1, zn)
            ]
        elif level == 4:
            for copy in state["s"]:
                copy.wait_recv()
            result = small_z[0]
            for z_at in range(1, zn):
                result = result + small_z[z_at]
            small_out[...] = result

    for tick in range(len(plan) + 6):
        for level in range(6, -1, -1):
            at = tick - level
            if 0 <= at < len(plan):
                stage(level, at)
        if tick < 5:
            small_stage(tick)
    sender.finish()


def reduce_plan(arrays, zn):
    plan = []
    for index, array in enumerate(arrays):
        rows, width = array.shape[0] // 4, array.shape[1]
        if width % (128 * zn) == 0:
            step = 1024 if width % 1024 == 0 else 512 if width % 512 == 0 else width
            plan += [(index, 0, rows, col, step, False) for col in range(0, width, step)]
        else:
            step = 256 if rows % 256 == 0 else rows
            plan += [(index, row, step, 0, width, True) for row in range(0, rows, step)]
    return plan


def reduce_weights(arrays, small, zn):
    plan = reduce_plan(arrays, zn)
    count = len(arrays)
    scratch = []
    for index, row, rows, col, width, by_rows in plan:
        half = rows // 2
        z_shape = (half // zn, width) if by_rows else (half, width // zn)
        scratch += [
            pltpu.VMEM((2, rows, width), BF),
            pltpu.VMEM((rows, width), BF),
            pltpu.VMEM((rows, width), BF),
            pltpu.VMEM((half, width), BF),
            pltpu.VMEM((zn - 1,) + z_shape, BF),
        ]
    copies = len(plan) * (5 + 2 * (zn - 1)) + 3 + zn - 1
    return pl.pallas_call(
        functools.partial(reduce_kernel, plan, count, zn),
        out_shape=[
            jax.ShapeDtypeStruct((array.shape[0] // 4, array.shape[1]), array.dtype)
            for array in arrays
        ]
        + [jax.ShapeDtypeStruct(small.shape, small.dtype)],
        in_specs=[pl.BlockSpec(memory_space=pltpu.VMEM)] * (count + 1),
        out_specs=[pl.BlockSpec(memory_space=pltpu.VMEM)] * (count + 1),
        scratch_shapes=scratch
        + [
            pltpu.VMEM((3,) + small.shape, F32),
            pltpu.VMEM((2,) + small.shape, F32),
            pltpu.VMEM((zn,) + small.shape, F32),
            pltpu.SemaphoreType.DMA((copies,)),
            pltpu.SemaphoreType.DMA((copies,)),
        ],
        compiler_params=pltpu.CompilerParams(
            collective_id=3, has_side_effects=True, vmem_limit_bytes=VMEM_LIMIT
        ),
    )(*arrays, small)


def shards(
    ctx_count,
    fsdp_count,
    tokens,
    positions,
    qkv_weight,
    out_weight,
    gate_up_weight,
    down_weight,
    norm_gains,
    qk_gains,
    cotangent,
):
    zn = ctx_count // 2
    own_kernels = fsdp_count == 4 and ctx_count == 8
    row_count = tokens.shape[1]
    all_places = positions[0]
    length = all_places.shape[0]
    places = lax.dynamic_slice_in_dim(all_places, lax.axis_index("ctx") * row_count, row_count, 0)
    weights = (qkv_weight, out_weight, gate_up_weight, down_weight)
    if own_kernels:
        qkv_full, out_full, gate_up_full, down_full = gather_weights(weights, zn)
    else:
        qkv_full, out_full, gate_up_full, down_full = [
            lax.all_gather(weight, "fsdp", axis=0, tiled=True) for weight in weights
        ]
    head_size = qk_gains.shape[1]
    query_width = out_full.shape[0]
    head_count = query_width // head_size
    hidden_size = down_full.shape[0]
    head_scale = head_size ** (-0.5)
    inputs_f = tokens[0].astype(F32)
    normed_in, inv_in = rms_forward(inputs_f, norm_gains[0])
    normed_in_b = normed_in.astype(BF)
    projected = nn(normed_in_b, qkv_full)
    query_pre = projected[:, :query_width].reshape(row_count, head_count, head_size)
    query_pre = query_pre.transpose(1, 0, 2)
    key_pre = projected[:, query_width : query_width + head_size]
    value_b = projected[:, query_width + head_size :].astype(BF)
    cosine, sine_part = rope_tables(places, head_size)
    query_norm, inv_query = rms_forward(query_pre, qk_gains[0])
    key_norm, inv_key = rms_forward(key_pre, qk_gains[1])
    query_b = (rotate(query_norm, cosine, sine_part) * head_scale).astype(BF)
    key_b = rotate(key_norm, cosine, sine_part).astype(BF)
    kv_b = jnp.concatenate([key_b, value_b], 1)
    if own_kernels:
        kv_all = gather_kv(kv_b, zn).reshape(length, 2 * head_size)
    else:
        kv_all = lax.all_gather(kv_b, "ctx", axis=0, tiled=True)
    key_all, value_all = kv_all[:, :head_size], kv_all[:, head_size:]
    query_rows = query_b.reshape(head_count * row_count, head_size)
    row_places = jnp.tile(places, head_count)
    visible = all_places[None, :] <= row_places[:, None]
    scores = jnp.where(visible, nt(query_rows, key_all), NEG)
    row_peak = jnp.max(scores, axis=1, keepdims=True)
    log_total = row_peak + jnp.log(jnp.sum(jnp.exp(scores - row_peak), axis=1, keepdims=True))
    probs_f = jnp.exp(scores - log_total)
    probs_b = probs_f.astype(BF)
    mixed_rows = nn(probs_b, value_all).astype(BF)

    def heads_in(rows):
        return rows.reshape(head_count, row_count, head_size)

    mixed_b = heads_in(mixed_rows).transpose(1, 0, 2).reshape(row_count, query_width)
    attn_out = nn(mixed_b, out_full)
    attn_norm, inv_attn = rms_forward(attn_out, norm_gains[1])
    resid = inputs_f + attn_norm
    normed_ff, inv_ff = rms_forward(resid, norm_gains[2])
    normed_ff_b = normed_ff.astype(BF)
    gate_up = nn(normed_ff_b, gate_up_full)
    gate_part = gate_up[:, :hidden_size]
    up_part = gate_up[:, hidden_size:]
    activated, gelu_pull = jax.vjp(gelu_tanh, gate_part)
    hidden_b = (activated * up_part).astype(BF)
    ffn_out = nn(hidden_b, down_full)
    ffn_norm, inv_out = rms_forward(ffn_out, norm_gains[3])
    output = resid + ffn_norm
    grad_f = cotangent[0].astype(F32)
    d_ffn, gain_three = rms_backward(ffn_out, inv_out, norm_gains[3], grad_f)
    d_ffn_b = d_ffn.astype(BF)
    grad_down_full = tn(hidden_b, d_ffn_b).astype(BF)
    d_hidden = nt(d_ffn_b, down_full)
    d_gate = gelu_pull(d_hidden * up_part)[0]
    d_gate_up_b = jnp.concatenate([d_gate, d_hidden * activated], 1).astype(BF)
    grad_gate_up_full = tn(normed_ff_b, d_gate_up_b).astype(BF)
    d_normed_ff = nt(d_gate_up_b, gate_up_full)
    d_resid_part, gain_two = rms_backward(resid, inv_ff, norm_gains[2], d_normed_ff)
    d_resid = grad_f + d_resid_part
    d_attn, gain_one = rms_backward(attn_out, inv_attn, norm_gains[1], d_resid)
    d_attn_b = d_attn.astype(BF)
    grad_out_full = tn(mixed_b, d_attn_b).astype(BF)
    d_mixed_b = nt(d_attn_b, out_full).astype(BF)
    d_mixed_rows = d_mixed_b.reshape(row_count, head_count, head_size).transpose(1, 0, 2)
    d_mixed_rows = d_mixed_rows.reshape(head_count * row_count, head_size)
    row_delta = jnp.sum(
        d_mixed_rows.astype(F32) * mixed_rows.astype(F32), axis=-1, keepdims=True
    )
    value_acc = tn(probs_b, d_mixed_rows)
    grad_probs = nt(d_mixed_rows, value_all)
    grad_scores = (probs_f * (grad_probs - row_delta)).astype(BF)
    d_query = heads_in(nn(grad_scores, key_all))
    key_acc = tn(grad_scores, query_rows)
    kv_acc = jnp.concatenate([key_acc, value_acc], 1)
    if own_kernels:
        kv_grad = reduce_kv(kv_acc.astype(BF).reshape(2 * zn, row_count, 2 * head_size), zn)
    else:
        kv_grad = lax.psum_scatter(kv_acc, "ctx", scatter_dimension=0, tiled=True)
    d_query_norm = rotate(d_query * head_scale, cosine, -sine_part)
    d_query_pre, gain_query = rms_backward(query_pre, inv_query, qk_gains[0], d_query_norm)
    d_key_norm = rotate(kv_grad[:, :head_size], cosine, -sine_part)
    d_key_pre, gain_key = rms_backward(key_pre, inv_key, qk_gains[1], d_key_norm)
    d_query_flat = d_query_pre.transpose(1, 0, 2).reshape(row_count, query_width)
    d_projected_b = jnp.concatenate([d_query_flat, d_key_pre, kv_grad[:, head_size:]], 1)
    d_projected_b = d_projected_b.astype(BF)
    grad_qkv_full = tn(normed_in_b, d_projected_b).astype(BF)
    d_normed_in = nt(d_projected_b, qkv_full)
    d_inputs, gain_zero = rms_backward(inputs_f, inv_in, norm_gains[0], d_normed_in)
    grad_tokens = d_resid + d_inputs
    gains_local = jnp.stack([gain_zero, gain_one, gain_two, gain_three], 0)
    qk_local = jnp.stack([gain_query, gain_key], 0)
    grads = (grad_down_full, grad_gate_up_full, grad_out_full, grad_qkv_full)
    if own_kernels:
        wide = norm_gains.shape[1] - head_size
        small = jnp.concatenate(
            [gains_local, jnp.pad(qk_local, ((0, 2), (0, wide)))], 0
        )
        grad_down, grad_gate_up, grad_out, grad_qkv, small = reduce_weights(grads, small, zn)
        gains_total, qk_total = small[:4], small[4:6, :head_size]
    else:
        parts = [lax.psum_scatter(grad, "fsdp", scatter_dimension=0, tiled=True) for grad in grads]
        parts = lax.psum([part.astype(F32) for part in parts], "ctx")
        grad_down, grad_gate_up, grad_out, grad_qkv = parts
        gains_total, qk_total = lax.psum((gains_local, qk_local), ("ctx", "fsdp"))
    return (
        output[None],
        grad_tokens[None],
        grad_qkv.astype(F32),
        grad_out.astype(F32),
        grad_gate_up.astype(F32),
        grad_down.astype(F32),
        gains_total,
        qk_total,
    )


def solution(mesh):
    in_specs = (
        P("fsdp", "ctx", None),
        P("fsdp", None),
        P("fsdp", None),
        P("fsdp", None),
        P("fsdp", None),
        P("fsdp", None),
        P(),
        P(),
        P("fsdp", "ctx", None),
    )
    out_specs = (
        P("fsdp", "ctx", None),
        P("fsdp", "ctx", None),
        P("fsdp", None),
        P("fsdp", None),
        P("fsdp", None),
        P("fsdp", None),
        P(),
        P(),
    )
    body = functools.partial(shards, mesh.shape["ctx"], mesh.shape["fsdp"])
    return jax.shard_map(body, mesh=mesh, in_specs=in_specs, out_specs=out_specs, check_vma=False)
```

time: 681 us -> 282 us (0.41)
  blocking collectives: 296 us -> 0 us
  waiting for transfers between devices: 268 us -> 0 us
  Pallas kernels: 0 us -> 212 us
  local copies, waits for them, and re-layouts: 41.8 us -> 11.5 us
  between operations: 20.6 us -> 1.61 us
    reduce_scatter x6 -> x0, waiting for transfers between devices: 253 us -> none  [the longest x1 60.5 us: shards(): lax.psum_scatter(value_acc[all_places], 'ctx', scatter_dimension=0, tiled...]
    psum x2 -> x0, blocking collectives: 233 us -> none  [the longest x1 222 us: shards(): lax.psum((grad_qkv_part, grad_out_part, grad_gate_up_part, grad_down_part...]
    pallas_call x0 -> x4, Pallas kernels: none -> 212 us  [the longest x1 108 us: reduce_weights(): pl.pallas_call(functools.partial(reduce_kernel, plan, count, zn), out_sha...]
    all_gather x2 -> x0, blocking collectives: 62.9 us -> none  [the longest x1 31.5 us: shards(): lax.all_gather(value_b, 'ctx', axis=0, tiled=True)]
    gather x4 -> x0, local copies, waits for them, and re-layouts: 17.2 us -> none  [the longest x1 4.7 us: shards(): key_acc[all_places]]
    all_gather x4 -> x0, waiting for transfers between devices: 13 us -> none  [the longest x1 12.6 us: shards(): lax.all_gather(qkv_weight, 'fsdp', axis=0, tiled=True)]
    convert_element_type x5 -> x8, other arithmetic: 1.77 us -> 8.68 us  [the longest x1 2.18 us: shards(): grad_qkv.astype(F32)]
    dot_general x33 -> x18, matrix products: 35.7 us -> 34.7 us  [the longest x6 14.2 us: tn(): lax.dot_general(left, right, (((0,), (0,)), ((), ())), preferred_element_...]
  transfers between devices with their start and end apart: 10 -> 0, of which waited for: 8 -> 0; matrix products, arithmetic and copies ran while one was open for 8% -> 0% of each run, Pallas kernels for 0% -> 0%
where the time goes in v1:
time: 282 us; the launch traced here: 281 us
  Pallas kernels  212 us (75%)
  matrix products  34.7 us (12%)
  other arithmetic  21.3 us (8%)
  local copies, waits for them, and re-layouts  11.5 us (4%)
    pallas_call x1, Pallas kernels, reduce_weights(): pl.pallas_call(functools.partial(reduce_kernel, plan, count, zn), out_sha...  108 us
    pallas_call x1, Pallas kernels, gather_weights(): pl.pallas_call(functools.partial(gather_kernel, plan, count, zn), out_sha...  58.4 us
    pallas_call x1, Pallas kernels, gather_kv(): pl.pallas_call(functools.partial(kv_gather_kernel, zn), out_shape=jax.Sha...  22.6 us
    pallas_call x1, Pallas kernels, reduce_kv(): pl.pallas_call(functools.partial(kv_reduce_kernel, zn), out_shape=jax.Sha...  22.4 us
    dot_general x6, matrix products, tn(): lax.dot_general(left, right, (((0,), (0,)), ((), ())), preferred_element_...  14.2 us
    dot_general x6, matrix products, nn(): return jnp.dot(left, right, preferred_element_type=F32)  11.1 us
    dot_general x6, matrix products, nt(): lax.dot_general(left, right, (((1,), (1,)), ((), ())), preferred_element_...  9.44 us

profile of v1, /device:TPU:0, one launch (start us, length us, event | category | flops | bytes accessed | tf_op | source)
XLA Modules:
  0.0 281.0 jit_solution(12682891072986267609)
XLA Ops:
  0.7 58.4 %shard_map.152 = (bf16[640,1536]{1,0:T(8,128)(2,1)}, bf16[1024,640]{1,0:T(8,128)(2,1)}, bf16[640,4096]{1,0:T(8,128)(2,1)}, bf16[2048,640]{1,0:T(8,128)(2,1)}) custom-call(bf16[160,1536]{1,0:T(8,128)(2,1)} %refs_0_.1, bf16[256,640]{1,0:T(8,128)(2,1)} %refs_1_.1, bf16[160,4096]{1,0:T(8,128)(2,1)} %refs_2_.1, bf16[512,640]{1,0:T(8,128)(2,1)} %refs_3_.1), custom_call_target="tpu_custom_call" | custom-call | tf_op jit(solution)/shard_map/pallas_call | solution.py:183
  59.1 0.6 add_reduce_fusion
  59.8 2.1 fusion.56
  62.0 0.2 reshape.187
  62.3 0.2 fusion.24
  62.5 0.2 fusion.37
  62.7 0.1 slice_negate_fusion.1
  63.1 0.3 multiply_cosine_fusion
  63.4 0.8 broadcast_multiply_fusion
  64.2 0.3 fusion.22
  64.6 0.7 pad_maximum_fusion.9.in_ref
  65.3 22.6 %shard_map.153 = bf16[8,128,512]{2,1,0:T(8,128)(2,1)} custom-call(bf16[128,512]{1,0:T(8,128)(2,1)} %pad_maximum_fusion.9.in_ref), custom_call_target="tpu_custom_call" | custom-call | tf_op jit(solution)/shard_map/pallas_call | solution.py:223
  88.0 1.7 fusion.5
  89.7 0.6 exponential_reduce_fusion
  90.3 0.6 convolution_convert_fusion.7
  90.9 0.2 copy.24
  91.1 1.9 multiply_reduce_fusion.9
  93.1 0.2 multiply_reduce_fusion.8
  93.3 3.5 %fusion.65 = f32[128,4096]{1,0:T(8,128)S(1)} fusion(bf16[640,4096]{1,0:T(8,128)(2,1)} %get-tuple-element.19, f32[128,640]{1,0:T(8,128)S(1)} %get-tuple-element.46, f32[640]{0:T(1024)S(1)} %get-tuple-element.41, f32[128]{0:T(128)S(1)} %add_rsqrt_fusion.2), kind=kOutput, calls=%fused_computation.154 | convolution fusion | flops 671334400 | bytes 7670784 | tf_op jit(solution)/shard_map/dot_general | solution.py:61
  96.8 0.4 multiply_convert_fusion.2
  97.2 1.3 copy-done.9
  98.6 0.7 multiply_reduce_fusion.7
  99.3 0.7 fusion.49
  100.0 0.9 fusion.40
  100.9 1.4 fusion.12
  102.4 0.5 slice-done.1
  102.8 2.3 multiply_reduce_fusion.3
  105.2 0.8 multiply_reduce_fusion.4
  106.0 0.7 copy-done.7
  106.8 0.1 multiply_convert_fusion.5
  106.9 0.5 convolution_convert_fusion.6
  107.6 0.2 multiply_reduce_fusion.2
  107.8 2.7 fusion
  110.5 2.3 copy.31
  112.8 2.5 convolution_convert_fusion.4
  115.3 2.3 copy.30
  117.6 1.8 convolution_convert_fusion.5
  119.4 1.1 pad_maximum_fusion.1.in_ref
  120.5 22.4 %shard_map.154 = f32[128,512]{1,0:T(8,128)} custom-call(bf16[8,128,512]{2,1,0:T(8,128)(2,1)} %pad_maximum_fusion.1.in_ref), custom_call_target="tpu_custom_call" | custom-call | tf_op jit(solution)/shard_map/pallas_call | solution.py:270
  142.9 0.9 slice.168
  143.8 0.9 slice_negate_fusion.3
  144.7 1.2 multiply_reduce_fusion.10
  145.9 1.0 multiply_convert_fusion.7
  146.9 2.4 fusion.18
  149.4 0.4 copy_multiply_fusion
  149.7 0.1 slice_negate_fusion
  149.9 0.4 copy-done.32
  150.3 0.9 multiply_reduce_fusion
  151.3 0.3 multiply_convert_fusion.4
  151.7 0.3 copy-done.13
  151.9 0.8 fusion.47
  152.8 0.9 fusion.46
  153.7 2.4 convolution_convert_fusion.2.refs_0_
  156.1 3.9 %convolution_convert_fusion.refs_1_ = bf16[640,4096]{1,0:T(8,128)(2,1)} fusion(bf16[128,2048]{1,0:T(8,128)(2,1)S(1)} %copy-done.31, bf16[128,2048]{1,0:T(8,128)(2,1)S(1)} %copy-done.29, f32[128,640]{1,0:T(8,128)S(1)} %get-tuple-element.46, f32[640]{0:T(1024)S(1)} %get-tuple-element.41, f32[128]{0:T(128)S(1)} %copy-done.51), kind=kOutput, calls=%fused_computation | convolution fusion | flops 676052992 | bytes 6622208 | tf_op jit(solution)/shard_map/dot_general | solution.py:57
  160.0 1.5 convolution_convert_fusion.3.refs_2_
  161.6 2.1 convolution_convert_fusion.1.refs_3_
  163.7 0.6 concatenate.51.refs_4_
  164.4 108.5 %shard_map.155 = (bf16[512,640]{1,0:T(8,128)(2,1)}, bf16[160,4096]{1,0:T(8,128)(2,1)}, bf16[256,640]{1,0:T(8,128)(2,1)}, bf16[160,1536]{1,0:T(8,128)(2,1)}, f32[8,640]{1,0:T(8,128)}) custom-call(bf16[2048,640]{1,0:T(8,128)(2,1)} %convolution_convert_fusion.2.refs_0_, bf16[640,4096]{1,0:T(8,128)(2,1)} %convolution_convert_fusion.refs_1_, ...), custom_call_target="tpu_custom_call" | custom-call | tf_op jit(solution)/shard_map/pallas_call | solution.py:447
  272.9 2.2 convert_element_type.119
  275.0 1.9 convert_element_type.120
  276.9 1.8 convert_element_type.121
  278.7 1.1 convert_element_type.122
  279.8 0.6 slice.108
  280.4 0.6 slice.109
  (150 shorter events, 1.1 us)
Async XLA Ops:
  0.6 58.4 %copy-start.52 = (f32[4,640]{1,0:T(4,128)S(1)}, f32[4,640]{1,0:T(4,128)}, u32[]{:S(2)}) copy-start(f32[4,640]{1,0:T(4,128)} %param.15) | copy-start | bytes 30724
  0.6 59.0 %copy-start.34 = (s32[1,1024]{1,0:T(1,128)S(1)}, s32[1,1024]{1,0:T(1,128)}, u32[]{:S(2)}) copy-start(s32[1,1024]{1,0:T(1,128)} %param.10) | copy-start | bytes 12292
  0.7 59.0 %copy-start.5 = (bf16[1,128,640]{2,1,0:T(8,128)(2,1)S(1)}, bf16[1,128,640]{2,1,0:T(8,128)(2,1)}, u32[]{:S(2)}) copy-start(bf16[1,128,640]{2,1,0:T(8,128)(2,1)} %param.9) | copy-start | bytes 491524
  59.7 30.6 %copy-start.36 = (s32[512]{0:T(512)}, s32[512]{0:T(512)S(1)}, u32[]{:S(2)}) copy-start(s32[512]{0:T(512)S(1)} %broadcast_bitcast_fusion) | copy-start | bytes 6148
  59.8 2.1 copy-start.56
  59.8 2.4 copy-start.59
  61.9 2.7 copy-start
  62.2 1.9 copy-start.41
  62.3 1.9 copy-start.39
  63.0 2.3 copy-start.53
  63.4 0.8 copy-start.26
  63.4 24.6 %copy-start.24 = (f32[128,128]{1,0:T(8,128)}, f32[128,128]{1,0:T(8,128)S(1)}, u32[]{:S(2)}) copy-start(f32[128,128]{1,0:T(8,128)S(1)} %get-tuple-element.70) | copy-start | bytes 196612
  64.6 25.1 %copy-start.18 = (bf16[4,128,256]{2,1,0:T(8,128)(2,1)}, bf16[4,128,256]{2,1,0:T(8,128)(2,1)S(1)}, u32[]{:S(2)}) copy-start(bf16[4,128,256]{2,1,0:T(8,128)(2,1)S(1)} %copy.23) | copy-start | bytes 786436
  88.0 2.3 copy-start.2
  90.3 0.8 copy-start.45
  90.9 2.3 copy-start.19
  91.1 1.9 copy-start.10
  93.3 11.9 %copy-start.50 = (f32[128]{0:T(128)}, f32[128]{0:T(128)S(1)}, u32[]{:S(2)}) copy-start(f32[128]{0:T(128)S(1)} %add_rsqrt_fusion.2) | copy-start | bytes 1540
  96.8 1.7 copy-start.9
  97.2 2.0 copy-start.14
  97.2 2.0 copy-start.35
  100.0 2.4 slice-start
  100.9 1.4 copy-start.21
  100.9 1.9 slice-start.1
  102.3 2.9 %copy-start.28 = (bf16[128,2048]{1,0:T(8,128)(2,1)}, bf16[128,2048]{1,0:T(8,128)(2,1)S(1)}, u32[]{:S(2)}) copy-start(bf16[128,2048]{1,0:T(8,128)(2,1)S(1)} %get-tuple-element.49) | copy-start | bytes 1572868
  102.3 2.9 %copy-start.30 = (bf16[128,2048]{1,0:T(8,128)(2,1)}, bf16[128,2048]{1,0:T(8,128)(2,1)S(1)}, u32[]{:S(2)}) copy-start(bf16[128,2048]{1,0:T(8,128)(2,1)S(1)} %get-tuple-element.50) | copy-start | bytes 1572868
  105.2 1.7 copy-start.1
  105.2 2.4 copy-start.20
  106.0 0.7 copy-start.7
  106.0 1.8 copy-start.3
  106.0 1.8 copy-start.37
  106.0 1.8 copy-start.46
  106.9 0.7 copy-start.15
  107.6 2.9 %copy-start.4 = (bf16[16,4,8,256]{3,2,0,1:T(8,128)(2,1)}, bf16[16,4,8,256]{3,2,0,1:T(8,128)(2,1)S(1)}, u32[]{:S(2)}) copy-start(bf16[16,4,8,256]{3,2,0,1:T(8,128)(2,1)S(1)} %copy.38) | copy-start | bytes 786436
  107.8 2.7 copy-start.43
  117.6 1.8 copy-start.12
  119.4 25.3 %copy-start.25 = (f32[128,128]{1,0:T(8,128)S(1)}, f32[128,128]{1,0:T(8,128)}, u32[]{:S(2)}) copy-start(f32[128,128]{1,0:T(8,128)} %copy-done.24) | copy-start | bytes 196612
  119.4 25.3 %copy-start.27 = (f32[128,128]{1,0:T(8,128)S(1)}, f32[128,128]{1,0:T(8,128)}, u32[]{:S(2)}) copy-start(f32[128,128]{1,0:T(8,128)} %copy-done.26) | copy-start | bytes 196612
  119.4 25.3 %copy-start.42 = (f32[1,256]{1,0:T(1,128)S(1)}, f32[1,256]{1,0:T(1,128)}, u32[]{:S(2)}) copy-start(f32[1,256]{1,0:T(1,128)} %copy-done.41) | copy-start | bytes 3076
  119.4 25.3 %copy-start.54 = (f32[128]{0:T(128)S(1)}, f32[128]{0:T(128)}, u32[]{:S(2)}) copy-start(f32[128]{0:T(128)} %copy-done.53) | copy-start | bytes 1540
  119.4 27.5 %copy-start.38 = (s32[512]{0:T(512)S(1)}, s32[512]{0:T(512)}, u32[]{:S(2)}) copy-start(s32[512]{0:T(512)} %copy-done.36) | copy-start | bytes 6148
  119.4 27.5 %copy-start.44 = (f32[512]{0:T(512)S(1)}, f32[512]{0:T(512)}, u32[]{:S(2)}) copy-start(f32[512]{0:T(512)} %copy-done.43) | copy-start | bytes 6148
  119.4 27.5 %copy-start.47 = (f32[512]{0:T(512)S(1)}, f32[512]{0:T(512)}, u32[]{:S(2)}) copy-start(f32[512]{0:T(512)} %copy-done.45) | copy-start | bytes 6148
  149.3 0.9 copy-start.32
  149.3 1.0 copy-start.33
  149.3 1.0 copy-start.40
  150.3 1.4 copy-start.6
  150.3 1.6 copy-start.13
  150.3 1.6 copy-start.57
  151.6 1.1 copy-start.8
  151.9 1.7 copy-start.22
  152.8 3.3 %copy-start.29 = (bf16[128,2048]{1,0:T(8,128)(2,1)S(1)}, bf16[128,2048]{1,0:T(8,128)(2,1)}, u32[]{:S(2)}) copy-start(bf16[128,2048]{1,0:T(8,128)(2,1)} %copy-done.28) | copy-start | bytes 1572868
  152.8 3.3 %copy-start.31 = (bf16[128,2048]{1,0:T(8,128)(2,1)S(1)}, bf16[128,2048]{1,0:T(8,128)(2,1)}, u32[]{:S(2)}) copy-start(bf16[128,2048]{1,0:T(8,128)(2,1)} %copy-done.30) | copy-start | bytes 1572868
  152.8 3.3 %copy-start.51 = (f32[128]{0:T(128)S(1)}, f32[128]{0:T(128)}, u32[]{:S(2)}) copy-start(f32[128]{0:T(128)} %copy-done.50) | copy-start | bytes 1540
  156.1 3.9 %copy-start.11 = (bf16[4,128,256]{1,2,0:T(8,128)(2,1)S(1)}, bf16[4,128,256]{1,2,0:T(8,128)(2,1)}, u32[]{:S(2)}) copy-start(bf16[4,128,256]{1,2,0:T(8,128)(2,1)} %copy-done.10) | copy-start | bytes 786436
  156.1 3.9 %copy-start.16 = (bf16[128,640]{1,0:T(8,128)(2,1)S(1)}, bf16[128,640]{1,0:T(8,128)(2,1)}, u32[]{:S(2)}) copy-start(bf16[128,640]{1,0:T(8,128)(2,1)} %copy-done.15) | copy-start | bytes 491524
  160.0 3.7 %copy-start.49 = (f32[640]{0:T(1024)S(1)}, f32[640]{0:T(1024)}, u32[]{:S(2)}) copy-start(f32[640]{0:T(1024)} %get-tuple-element.32) | copy-start | bytes 7684
  160.0 3.7 %copy-start.58 = (f32[640]{0:T(1024)S(1)}, f32[640]{0:T(1024)}, u32[]{:S(2)}) copy-start(f32[640]{0:T(1024)} %get-tuple-element.30) | copy-start | bytes 7684
  160.0 3.7 %copy-start.48 = (f32[640]{0:T(1024)S(1)}, f32[640]{0:T(1024)}, u32[]{:S(2)}) copy-start(f32[640]{0:T(1024)} %get-tuple-element.34) | copy-start | bytes 7684
  272.8 4.0 %copy-start.17 = (bf16[160,4096]{1,0:T(8,128)(2,1)S(1)}, bf16[160,4096]{1,0:T(8,128)(2,1)}, u32[]{:S(2)}) copy-start(bf16[160,4096]{1,0:T(8,128)(2,1)} %get-tuple-element.23) | copy-start | bytes 3932164
  276.9 1.8 copy-start.23
  276.9 2.9 %copy-start.55 = (f32[8,640]{1,0:T(8,128)S(1)}, f32[8,640]{1,0:T(8,128)}, u32[]{:S(2)}) copy-start(f32[8,640]{1,0:T(8,128)} %get-tuple-element.25) | copy-start | bytes 61444

commit v2 on v1

--- a/solution.py
+++ b/solution.py
@@ -116,13 +116,24 @@
     return pl.ds(pl.multiple_of(start, 16), size)
 
 
-def gather_kernel(plan, count, zn, *refs):
-    ins, outs = refs[:count], refs[count : 2 * count]
-    send_sem, recv_sem, own_sem = refs[2 * count :]
+def gather_kernel(plan, count, with_kv, zn, *refs):
+    total = count + with_kv
+    ins, outs = refs[:total], refs[total : 2 * total]
+    send_sem, recv_sem, own_sem = refs[2 * total :]
     here = Place(zn)
-    greet([here.core_peer, here.x_peer, here.y_peer])
+    peers = [here.core_peer, here.x_peer, here.y_peer]
+    greet(peers + [here.z_peer(step) for step in range(1, zn)] * with_kv)
     sender = Sender(send_sem, recv_sem)
     own_copies = []
+    if with_kv:
+        kv_in, kv_out = ins[count], outs[count]
+        along_z = [
+            sender.start(kv_in, kv_out.at[here.ctx], here.z_peer(step)) for step in range(1, zn)
+        ]
+        along_y = [sender.start(kv_in, kv_out.at[here.ctx], here.y_peer)]
+        own_kv = pltpu.make_async_copy(kv_in, kv_out.at[here.ctx], own_sem.at[len(plan)])
+        own_kv.start()
+        own_copies.append(own_kv)
     state = {}
 
     def spot(chunk, quarter, half):
@@ -168,127 +179,46 @@
             at = tick - (level - 1)
             if 0 <= at < len(plan):
                 stage(level, at)
+        if with_kv and tick < zn - 1:
+            along_z[tick].wait_recv()
+            block = kv_out.at[here.z_index(zn - 1 - tick) * 2 + here.y]
+            along_y.append(sender.start(block, block, here.y_peer))
+    if with_kv:
+        for copy in along_y:
+            copy.wait_recv()
     for own in own_copies:
         own.wait()
     sender.finish()
 
 
-def gather_weights(arrays, zn):
+def gather_weights(arrays, kv, zn):
     plan = []
     for index, array in enumerate(arrays):
         width = array.shape[1]
-        step = width if width <= 1536 else 1024
+        step = 1024 if width % 1024 == 0 else 768 if width % 768 == 0 else width
         plan += [(index, col, step) for col in range(0, width, step)]
     count = len(arrays)
+    assert len(plan) + 2 >= zn - 1
+    shapes = [((4 * array.shape[0], array.shape[1]), array.dtype) for array in arrays]
+    shapes += [((2 * zn,) + block.shape, block.dtype) for block in kv]
+    copies = 5 * len(plan) + len(kv) * (2 * zn - 1)
     return pl.pallas_call(
-        functools.partial(gather_kernel, plan, count, zn),
-        out_shape=[
-            jax.ShapeDtypeStruct((4 * array.shape[0], array.shape[1]), array.dtype)
-            for array in arrays
-        ],
-        in_specs=[pl.BlockSpec(memory_space=pltpu.VMEM)] * count,
-        out_specs=[pl.BlockSpec(memory_space=pltpu.VMEM)] * count,
+        functools.partial(gather_kernel, plan, count, len(kv), zn),
+        out_shape=[jax.ShapeDtypeStruct(*shape) for shape in shapes],
+        in_specs=[pl.BlockSpec(memory_space=pltpu.VMEM)] * (count + len(kv)),
+        out_specs=[pl.BlockSpec(memory_space=pltpu.VMEM)] * (count + len(kv)),
         scratch_shapes=[
-            pltpu.SemaphoreType.DMA((5 * len(plan),)),
-            pltpu.SemaphoreType.DMA((5 * len(plan),)),
-            pltpu.SemaphoreType.DMA((len(plan),)),
+            pltpu.SemaphoreType.DMA((copies,)),
+            pltpu.SemaphoreType.DMA((copies,)),
+            pltpu.SemaphoreType.DMA((len(plan) + len(kv),)),
         ],
         compiler_params=pltpu.CompilerParams(
-            collective_id=0, has_side_effects=True, vmem_limit_bytes=VMEM_LIMIT
+            collective_id=len(kv), has_side_effects=True, vmem_limit_bytes=VMEM_LIMIT
         ),
-    )(*arrays)
-
-
-def kv_gather_kernel(zn, in_ref, out_ref, send_sem, recv_sem, own_sem):
-    here = Place(zn)
-    greet([here.y_peer] + [here.z_peer(step) for step in range(1, zn)])
-    sender = Sender(send_sem, recv_sem)
-    along_z = [
-        sender.start(in_ref, out_ref.at[here.ctx], here.z_peer(step)) for step in range(1, zn)
-    ]
-    along_y = [sender.start(in_ref, out_ref.at[here.ctx], here.y_peer)]
-    own = pltpu.make_async_copy(in_ref, out_ref.at[here.ctx], own_sem.at[0])
-    own.start()
-    for step in range(1, zn):
-        along_z[step - 1].wait_recv()
-        block = out_ref.at[here.z_index(zn - step) * 2 + here.y]
-        along_y.append(sender.start(block, block, here.y_peer))
-    for copy in along_y:
-        copy.wait_recv()
-    own.wait()
-    sender.finish()
-
-
-def gather_kv(block, zn):
-    return pl.pallas_call(
-        functools.partial(kv_gather_kernel, zn),
-        out_shape=jax.ShapeDtypeStruct((2 * zn,) + block.shape, block.dtype),
-        in_specs=[pl.BlockSpec(memory_space=pltpu.VMEM)],
-        out_specs=pl.BlockSpec(memory_space=pltpu.VMEM),
-        scratch_shapes=[
-            pltpu.SemaphoreType.DMA((2 * zn - 1,)),
-            pltpu.SemaphoreType.DMA((2 * zn - 1,)),
-            pltpu.SemaphoreType.DMA((1,)),
-        ],
-        compiler_params=pltpu.CompilerParams(
-            collective_id=1, has_side_effects=True, vmem_limit_bytes=VMEM_LIMIT
-        ),
-    )(block)
-
-
-def kv_reduce_kernel(zn, in_ref, out_ref, from_y, summed, from_z, send_sem, recv_sem):
-    here = Place(zn)
-    greet([here.y_peer] + [here.z_peer(step) for step in range(1, zn)])
-    sender = Sender(send_sem, recv_sem)
-    order = list(range(1, zn)) + [0]
-    along_y = []
-    for step in order:
-        target = here.z_index(step)
-        along_y.append(
-            sender.start(in_ref.at[target * 2 + 1 - here.y], from_y.at[target], here.y_peer)
-        )
-    along_z = []
-    for at, step in enumerate(order):
-        along_y[at].wait_recv()
-        target = here.z_index(step)
-        both = in_ref[target * 2 + here.y].astype(F32) + from_y[target].astype(F32)
-        if step == 0:
-            out_ref[...] = both
-        else:
-            summed[step - 1] = both.astype(BF)
-            along_z.append(
-                sender.start(summed.at[step - 1], from_z.at[step - 1], here.z_peer(step))
-            )
-    for step in range(1, zn):
-        along_z[step - 1].wait_recv()
-        out_ref[...] += from_z[step - 1].astype(F32)
-    sender.finish()
-
-
-def reduce_kv(blocks, zn):
-    shape = blocks.shape[1:]
-    return pl.pallas_call(
-        functools.partial(kv_reduce_kernel, zn),
-        out_shape=jax.ShapeDtypeStruct(shape, F32),
-        in_specs=[pl.BlockSpec(memory_space=pltpu.VMEM)],
-        out_specs=pl.BlockSpec(memory_space=pltpu.VMEM),
-        scratch_shapes=[
-            pltpu.VMEM((zn,) + shape, BF),
-            pltpu.VMEM((zn - 1,) + shape, BF),
-            pltpu.VMEM((zn - 1,) + shape, BF),
-            pltpu.SemaphoreType.DMA((2 * zn - 1,)),
-            pltpu.SemaphoreType.DMA((2 * zn - 1,)),
-        ],
-        compiler_params=pltpu.CompilerParams(
-            collective_id=2, has_side_effects=True, vmem_limit_bytes=VMEM_LIMIT
-        ),
-    )(blocks)
-
-
-PER_CHUNK = 11
-
-
-def reduce_kernel(plan, count, zn, *refs):
+    )(*arrays, *kv)
+
+
+def reduce_kernel(plan, count, with_kv, zn, *refs):
     ins, small_in = refs[:count], refs[count]
     outs, small_out = refs[count + 1 : 2 * count + 1], refs[2 * count + 1]
     rest = refs[2 * count + 2 :]
@@ -329,7 +259,6 @@
         mine = rows_at(here.y * half, half)
         other = rows_at((1 - here.y) * half, half)
         if level == 0:
-            order = (1 - here.x, here.x)
             state[at] = [
                 sender.start(
                     block(ins[index], chunk, side * 2 + 1 - here.c),
@@ -406,13 +335,45 @@
                 result = result + small_z[z_at]
             small_out[...] = result
 
+    order_z = list(range(1, zn)) + [0]
+
+    def kv_stage(level):
+        if level == 0:
+            state["y"] = []
+            state["z"] = []
+            for step in order_z:
+                target = here.z_index(step)
+                state["y"].append(
+                    sender.start(
+                        small_in.at[target * 2 + 1 - here.y], small_recv.at[target], here.y_peer
+                    )
+                )
+        elif level == 1:
+            for at, step in enumerate(order_z):
+                state["y"][at].wait_recv()
+                target = here.z_index(step)
+                both = small_in[target * 2 + here.y].astype(F32) + small_recv[target].astype(F32)
+                if step == 0:
+                    small_out[...] = both
+                else:
+                    small_sum[step - 1] = both.astype(BF)
+                    state["z"].append(
+                        sender.start(
+                            small_sum.at[step - 1], small_z.at[step - 1], here.z_peer(step)
+                        )
+                    )
+        elif level == 4:
+            for step in range(1, zn):
+                state["z"][step - 1].wait_recv()
+                small_out[...] += small_z[step - 1].astype(F32)
+
     for tick in range(len(plan) + 6):
         for level in range(6, -1, -1):
             at = tick - level
             if 0 <= at < len(plan):
                 stage(level, at)
         if tick < 5:
-            small_stage(tick)
+            (kv_stage if with_kv else small_stage)(tick)
     sender.finish()
 
 
@@ -421,15 +382,24 @@
     for index, array in enumerate(arrays):
         rows, width = array.shape[0] // 4, array.shape[1]
         if width % (128 * zn) == 0:
-            step = 1024 if width % 1024 == 0 else 512 if width % 512 == 0 else width
-            plan += [(index, 0, rows, col, step, False) for col in range(0, width, step)]
+            step = 128 * zn
+            cols = list(range(0, width, step))
+            if len(cols) >= 6:
+                cols = [0] + cols[1:-1:2] + [width - step]
+            ends = cols[1:] + [width]
+            plan += [
+                (index, 0, rows, col, end - col, False) for col, end in zip(cols, ends)
+            ]
         else:
             step = 256 if rows % 256 == 0 else rows
             plan += [(index, row, step, 0, width, True) for row in range(0, rows, step)]
+    wide = [at for at, chunk in enumerate(plan) if not chunk[5]]
+    if wide:
+        plan = [plan[wide[0]]] + plan[: wide[0]] + plan[wide[0] + 1 :]
     return plan
 
 
-def reduce_weights(arrays, small, zn):
+def reduce_weights(arrays, small, with_kv, zn):
     plan = reduce_plan(arrays, zn)
     count = len(arrays)
     scratch = []
@@ -443,26 +413,37 @@
             pltpu.VMEM((half, width), BF),
             pltpu.VMEM((zn - 1,) + z_shape, BF),
         ]
-    copies = len(plan) * (5 + 2 * (zn - 1)) + 3 + zn - 1
+    copies = len(plan) * (5 + 2 * (zn - 1)) + 2 * zn + 2
+    if with_kv:
+        shape = small.shape[1:]
+        scratch += [
+            pltpu.VMEM((zn,) + shape, BF),
+            pltpu.VMEM((zn - 1,) + shape, BF),
+            pltpu.VMEM((zn - 1,) + shape, BF),
+        ]
+    else:
+        shape = small.shape
+        scratch += [
+            pltpu.VMEM((3,) + shape, F32),
+            pltpu.VMEM((2,) + shape, F32),
+            pltpu.VMEM((zn,) + shape, F32),
+        ]
     return pl.pallas_call(
-        functools.partial(reduce_kernel, plan, count, zn),
+        functools.partial(reduce_kernel, plan, count, with_kv, zn),
         out_shape=[
             jax.ShapeDtypeStruct((array.shape[0] // 4, array.shape[1]), array.dtype)
             for array in arrays
         ]
-        + [jax.ShapeDtypeStruct(small.shape, small.dtype)],
+        + [jax.ShapeDtypeStruct(shape, F32)],
         in_specs=[pl.BlockSpec(memory_space=pltpu.VMEM)] * (count + 1),
         out_specs=[pl.BlockSpec(memory_space=pltpu.VMEM)] * (count + 1),
         scratch_shapes=scratch
         + [
-            pltpu.VMEM((3,) + small.shape, F32),
-            pltpu.VMEM((2,) + small.shape, F32),
-            pltpu.VMEM((zn,) + small.shape, F32),
             pltpu.SemaphoreType.DMA((copies,)),
             pltpu.SemaphoreType.DMA((copies,)),
         ],
         compiler_params=pltpu.CompilerParams(
-            collective_id=3, has_side_effects=True, vmem_limit_bytes=VMEM_LIMIT
+            collective_id=2 + with_kv, has_side_effects=True, vmem_limit_bytes=VMEM_LIMIT
         ),
     )(*arrays, small)
 
@@ -486,17 +467,15 @@
     all_places = positions[0]
     length = all_places.shape[0]
     places = lax.dynamic_slice_in_dim(all_places, lax.axis_index("ctx") * row_count, row_count, 0)
-    weights = (qkv_weight, out_weight, gate_up_weight, down_weight)
+    weights = (out_weight, down_weight, gate_up_weight)
     if own_kernels:
-        qkv_full, out_full, gate_up_full, down_full = gather_weights(weights, zn)
+        (qkv_full,) = gather_weights((qkv_weight,), (), zn)
     else:
-        qkv_full, out_full, gate_up_full, down_full = [
-            lax.all_gather(weight, "fsdp", axis=0, tiled=True) for weight in weights
-        ]
+        qkv_full = lax.all_gather(qkv_weight, "fsdp", axis=0, tiled=True)
     head_size = qk_gains.shape[1]
-    query_width = out_full.shape[0]
+    query_width = out_weight.shape[0] * fsdp_count
     head_count = query_width // head_size
-    hidden_size = down_full.shape[0]
+    hidden_size = down_weight.shape[0] * fsdp_count
     head_scale = head_size ** (-0.5)
     inputs_f = tokens[0].astype(F32)
     normed_in, inv_in = rms_forward(inputs_f, norm_gains[0])
@@ -513,8 +492,12 @@
     key_b = rotate(key_norm, cosine, sine_part).astype(BF)
     kv_b = jnp.concatenate([key_b, value_b], 1)
     if own_kernels:
-        kv_all = gather_kv(kv_b, zn).reshape(length, 2 * head_size)
+        out_full, down_full, gate_up_full, kv_all = gather_weights(weights, (kv_b,), zn)
+        kv_all = kv_all.reshape(length, 2 * head_size)
     else:
+        out_full, down_full, gate_up_full = [
+            lax.all_gather(weight, "fsdp", axis=0, tiled=True) for weight in weights
+        ]
         kv_all = lax.all_gather(kv_b, "ctx", axis=0, tiled=True)
     key_all, value_all = kv_all[:, :head_size], kv_all[:, head_size:]
     query_rows = query_b.reshape(head_count * row_count, head_size)
@@ -571,7 +554,9 @@
     key_acc = tn(grad_scores, query_rows)
     kv_acc = jnp.concatenate([key_acc, value_acc], 1)
     if own_kernels:
-        kv_grad = reduce_kv(kv_acc.astype(BF).reshape(2 * zn, row_count, 2 * head_size), zn)
+        kv_parts = kv_acc.astype(BF).reshape(2 * zn, row_count, 2 * head_size)
+        grads = (grad_down_full, grad_out_full, grad_gate_up_full)
+        grad_down, grad_out, grad_gate_up, kv_grad = reduce_weights(grads, kv_parts, 1, zn)
     else:
         kv_grad = lax.psum_scatter(kv_acc, "ctx", scatter_dimension=0, tiled=True)
     d_query_norm = rotate(d_query * head_scale, cosine, -sine_part)
@@ -587,15 +572,15 @@
     grad_tokens = d_resid + d_inputs
     gains_local = jnp.stack([gain_zero, gain_one, gain_two, gain_three], 0)
     qk_local = jnp.stack([gain_query, gain_key], 0)
-    grads = (grad_down_full, grad_gate_up_full, grad_out_full, grad_qkv_full)
     if own_kernels:
         wide = norm_gains.shape[1] - head_size
         small = jnp.concatenate(
             [gains_local, jnp.pad(qk_local, ((0, 2), (0, wide)))], 0
         )
-        grad_down, grad_gate_up, grad_out, grad_qkv, small = reduce_weights(grads, small, zn)
+        grad_qkv, small = reduce_weights((grad_qkv_full,), small, 0, zn)
         gains_total, qk_total = small[:4], small[4:6, :head_size]
     else:
+        grads = (grad_down_full, grad_gate_up_full, grad_out_full, grad_qkv_full)
         parts = [lax.psum_scatter(grad, "fsdp", scatter_dimension=0, tiled=True) for grad in grads]
         parts = lax.psum([part.astype(F32) for part in parts], "ctx")
         grad_down, grad_gate_up, grad_out, grad_qkv = parts

time: 282 us -> 279 us (0.989)
  matrix products: 34.7 us -> 31.7 us
where the time goes in v2:
time: 279 us; the launch traced here: 278 us
  Pallas kernels  211 us (76%)
  matrix products  31.7 us (11%)
  other arithmetic  23.4 us (8%)
  local copies, waits for them, and re-layouts  10.6 us (4%)
    pallas_call x2, Pallas kernels, reduce_weights(): pl.pallas_call(functools.partial(reduce_kernel, plan, count, with_kv, zn)...  134 us
    pallas_call x2, Pallas kernels, gather_weights(): pl.pallas_call(functools.partial(gather_kernel, plan, count, len(kv), zn)...  76.7 us
    dot_general x6, matrix products, tn(): lax.dot_general(left, right, (((0,), (0,)), ((), ())), preferred_element_...  13.4 us
    dot_general x6, matrix products, nn(): return jnp.dot(left, right, preferred_element_type=F32)  9.51 us
    dot_general x6, matrix products, nt(): lax.dot_general(left, right, (((1,), (1,)), ((), ())), preferred_element_...  8.85 us

profile of v2, /device:TPU:0, one launch (start us, length us, event | category | flops | bytes accessed | tf_op | source)
XLA Modules:
  0.0 277.9 jit_solution(13940870481489937126)
XLA Ops:
  0.6 1.5 add_reduce_fusion
  2.1 1.0 fusion.48
  3.2 20.4 %shard_map.152 = bf16[640,1536]{1,0:T(8,128)(2,1)} custom-call(bf16[160,1536]{1,0:T(8,128)(2,1)} %refs_0_.2), custom_call_target="tpu_custom_call" | custom-call | tf_op jit(solution)/shard_map/pallas_call | solution.py:205
  23.7 2.1 fusion.56
  26.1 0.3 multiply_cosine_fusion
  26.4 0.8 broadcast_multiply_fusion
  27.2 0.2 reshape.187
  27.5 0.2 fusion.24
  27.7 0.2 fusion.37
  27.9 0.1 slice_negate_fusion.1
  28.1 0.3 fusion.22
  28.5 0.7 pad_maximum_fusion.9.refs_3_
  29.2 56.3 %shard_map.153 = (bf16[1024,640]{1,0:T(8,128)(2,1)}, bf16[2048,640]{1,0:T(8,128)(2,1)}, bf16[640,4096]{1,0:T(8,128)(2,1)}, bf16[8,128,512]{2,1,0:T(8,128)(2,1)}) custom-call(bf16[256,640]{1,0:T(8,128)(2,1)} %refs_0_.3, bf16[512,640]{1,0:T(8,128)(2,1)} %refs_1_.1, bf16[160,4096]{1,0:T(8,128)(2,1)} %refs_2_.1, bf16[128,512]{1,0:T(8,128)(2,1)} %pad_maximum_fusion.9.refs_3_), custom_call_target="tpu_custom_call" | custom-call | tf_op jit(solution)/shard_map/pallas_call | solution.py:205
  85.5 1.7 fusion.5
  87.2 0.6 exponential_reduce_fusion
  87.8 0.6 convolution_convert_fusion.7
  88.5 0.2 copy.24
  88.7 1.9 multiply_reduce_fusion.9
  90.6 0.2 multiply_reduce_fusion.8
  90.8 3.5 %fusion.65 = f32[128,4096]{1,0:T(8,128)S(1)} fusion(bf16[640,4096]{1,0:T(8,128)(2,1)} %get-tuple-element.20, f32[128,640]{1,0:T(8,128)S(1)} %get-tuple-element.48, f32[640]{0:T(1024)S(1)} %get-tuple-element.43, f32[128]{0:T(128)S(1)} %add_rsqrt_fusion.2), kind=kOutput, calls=%fused_computation.154 | convolution fusion | flops 671334400 | bytes 7670784 | tf_op jit(solution)/shard_map/dot_general | solution.py:61
  94.4 0.4 multiply_convert_fusion.2
  94.8 1.3 copy-done.12
  96.1 0.7 multiply_reduce_fusion.7
  96.8 0.7 fusion.49
  97.5 0.9 fusion.40
  98.4 1.4 fusion.12
  99.9 0.5 slice-done.1
  100.4 2.4 multiply_reduce_fusion.3
  102.8 0.8 multiply_reduce_fusion.4
  103.6 0.7 copy-done.10
  104.3 0.1 multiply_convert_fusion.5
  104.5 0.5 convolution_convert_fusion.6
  105.1 0.2 multiply_reduce_fusion.2
  105.3 2.1 fusion
  107.3 0.8 fusion.18
  108.1 0.4 copy_multiply_fusion
  108.5 0.1 slice_negate_fusion
  108.6 0.4 copy-done.36
  109.1 2.2 multiply_reduce_fusion
  111.3 1.3 copy.30
  112.6 1.7 convolution_convert_fusion.5
  114.3 1.3 copy.31
  115.7 1.7 convolution_convert_fusion.4
  117.4 1.0 pad_maximum_fusion.1.refs_3_
  118.5 3.9 %convolution_convert_fusion.refs_2_ = bf16[640,4096]{1,0:T(8,128)(2,1)} fusion(bf16[128,2048]{1,0:T(8,128)(2,1)S(1)} %copy-done.35, bf16[128,2048]{1,0:T(8,128)(2,1)S(1)} %copy-done.33, f32[128,640]{1,0:T(8,128)S(1)} %get-tuple-element.48, f32[640]{0:T(1024)S(1)} %get-tuple-element.43, f32[128]{0:T(128)S(1)} %copy-done.53), kind=kOutput, calls=%fused_computation | convolution fusion | flops 676052992 | bytes 6622208 | tf_op jit(solution)/shard_map/dot_general | solution.py:57
  122.4 1.5 convolution_convert_fusion.3.refs_1_
  124.0 2.4 convolution_convert_fusion.2.refs_0_
  126.4 94.6 %shard_map.154 = (bf16[512,640]{1,0:T(8,128)(2,1)}, bf16[256,640]{1,0:T(8,128)(2,1)}, bf16[160,4096]{1,0:T(8,128)(2,1)}, f32[128,512]{1,0:T(8,128)}) custom-call(bf16[2048,640]{1,0:T(8,128)(2,1)} %convolution_convert_fusion.2.refs_0_, bf16[1024,640]{1,0:T(8,128)(2,1)} %convolution_convert_fusion.3.refs_1_, ...), custom_call_target="tpu_custom_call" | custom-call | tf_op jit(solution)/shard_map/pallas_call | solution.py:431
  221.0 1.0 slice_negate_fusion.3
  222.1 1.2 multiply_reduce_fusion.10
  223.3 0.3 multiply_convert_fusion.4
  223.7 1.0 multiply_convert_fusion.7
  224.7 0.9 slice.168
  225.7 0.8 fusion.47
  226.6 0.6 concatenate.51.refs_1_
  227.2 2.0 convolution_convert_fusion.1.refs_0_
  229.3 39.3 %shard_map.155 = (bf16[160,1536]{1,0:T(8,128)(2,1)}, f32[8,640]{1,0:T(8,128)}) custom-call(bf16[640,1536]{1,0:T(8,128)(2,1)} %convolution_convert_fusion.1.refs_0_, f32[8,640]{1,0:T(8,128)} %concatenate.51.refs_1_), custom_call_target="tpu_custom_call" | custom-call | tf_op jit(solution)/shard_map/pallas_call | solution.py:431
  268.5 2.1 convert_element_type.119
  270.6 1.3 slice.108
  271.9 1.3 slice.109
  273.2 0.9 fusion.46
  274.1 1.8 convert_element_type.121
  275.9 1.1 convert_element_type.122
  277.0 0.9 convert_element_type.120
  (150 shorter events, 0.9 us)
Async XLA Ops:
  0.6 23.0 %copy-start.7 = (bf16[1,128,640]{2,1,0:T(8,128)(2,1)S(1)}, bf16[1,128,640]{2,1,0:T(8,128)(2,1)}, u32[]{:S(2)}) copy-start(bf16[1,128,640]{2,1,0:T(8,128)(2,1)} %param.9) | copy-start | bytes 491524
  3.2 22.6 %copy-start.56 = (f32[128]{0:T(128)}, f32[128]{0:T(128)S(1)}, u32[]{:S(2)}) copy-start(f32[128]{0:T(128)S(1)} %add_rsqrt_fusion.5) | copy-start | bytes 1540
  23.6 2.2 copy-start.59
  23.6 2.4 copy-start.40
  25.7 2.7 copy-start.1
  25.9 1.3 copy-start.54
  25.9 1.3 copy-start.44
  25.9 2.2 copy-start.46
  26.4 0.8 copy-start.28
  26.4 0.8 copy-start.30
  28.5 58.7 %copy-start.22 = (bf16[4,128,256]{2,1,0:T(8,128)(2,1)}, bf16[4,128,256]{2,1,0:T(8,128)(2,1)S(1)}, u32[]{:S(2)}) copy-start(bf16[4,128,256]{2,1,0:T(8,128)(2,1)S(1)} %copy.23) | copy-start | bytes 786436
  85.5 2.3 copy-start.42
  85.5 2.3 copy-start.20
  87.8 0.8 copy-start.48
  88.4 2.4 copy-start.23
  88.4 2.1 copy-start.8
  88.6 1.9 copy-start.13
  90.8 11.9 %copy-start.52 = (f32[128]{0:T(128)}, f32[128]{0:T(128)S(1)}, u32[]{:S(2)}) copy-start(f32[128]{0:T(128)S(1)} %add_rsqrt_fusion.2) | copy-start | bytes 1540
  94.3 1.7 copy-start.12
  94.7 2.0 copy-start.16
  94.7 2.0 copy-start.41
  97.5 2.4 slice-start
  98.4 1.4 copy-start.25
  98.4 1.9 slice-start.1
  99.8 2.9 %copy-start.32 = (bf16[128,2048]{1,0:T(8,128)(2,1)}, bf16[128,2048]{1,0:T(8,128)(2,1)S(1)}, u32[]{:S(2)}) copy-start(bf16[128,2048]{1,0:T(8,128)(2,1)S(1)} %get-tuple-element.51) | copy-start | bytes 1572868
  99.8 2.9 %copy-start.34 = (bf16[128,2048]{1,0:T(8,128)(2,1)}, bf16[128,2048]{1,0:T(8,128)(2,1)S(1)}, u32[]{:S(2)}) copy-start(bf16[128,2048]{1,0:T(8,128)(2,1)S(1)} %get-tuple-element.52) | copy-start | bytes 1572868
  102.7 1.7 copy-start.2
  102.8 2.3 copy-start.24
  103.6 0.7 copy-start.10
  103.6 1.7 copy-start.21
  103.6 1.7 copy-start.43
  103.6 1.7 copy-start.49
  104.4 0.8 copy-start.17
  105.0 2.3 copy-start.5
  108.1 0.9 copy-start.36
  108.1 1.0 copy-start.37
  108.1 1.0 copy-start.47
  108.1 3.1 %copy-start.4 = (bf16[1024,512]{0,1:T(8,128)(2,1)S(1)}, bf16[1024,512]{0,1:T(8,128)(2,1)}, u32[]{:S(2)}) copy-start(bf16[1024,512]{0,1:T(8,128)(2,1)} %get-tuple-element.53) | copy-start | bytes 3145732
  111.3 3.1 %copy-start.3 = (bf16[1024,512]{0,1:T(8,128)(2,1)S(1)}, bf16[1024,512]{0,1:T(8,128)(2,1)}, u32[]{:S(2)}) copy-start(bf16[1024,512]{0,1:T(8,128)(2,1)} %get-tuple-element.54) | copy-start | bytes 3145732
  112.6 3.1 %copy-start.6 = (bf16[16,4,8,256]{3,2,0,1:T(8,128)(2,1)S(1)}, bf16[16,4,8,256]{3,2,0,1:T(8,128)(2,1)}, u32[]{:S(2)}) copy-start(bf16[16,4,8,256]{3,2,0,1:T(8,128)(2,1)} %copy-done.5) | copy-start | bytes 786436
  115.7 2.8 %copy-start.33 = (bf16[128,2048]{1,0:T(8,128)(2,1)S(1)}, bf16[128,2048]{1,0:T(8,128)(2,1)}, u32[]{:S(2)}) copy-start(bf16[128,2048]{1,0:T(8,128)(2,1)} %copy-done.32) | copy-start | bytes 1572868
  115.7 2.8 %copy-start.35 = (bf16[128,2048]{1,0:T(8,128)(2,1)S(1)}, bf16[128,2048]{1,0:T(8,128)(2,1)}, u32[]{:S(2)}) copy-start(bf16[128,2048]{1,0:T(8,128)(2,1)} %copy-done.34) | copy-start | bytes 1572868
  115.7 2.8 %copy-start.53 = (f32[128]{0:T(128)S(1)}, f32[128]{0:T(128)}, u32[]{:S(2)}) copy-start(f32[128]{0:T(128)} %copy-done.52) | copy-start | bytes 1540
  118.5 3.9 %copy-start.14 = (bf16[4,128,256]{1,2,0:T(8,128)(2,1)S(1)}, bf16[4,128,256]{1,2,0:T(8,128)(2,1)}, u32[]{:S(2)}) copy-start(bf16[4,128,256]{1,2,0:T(8,128)(2,1)} %copy-done.13) | copy-start | bytes 786436
  118.5 3.9 %copy-start.18 = (bf16[128,640]{1,0:T(8,128)(2,1)S(1)}, bf16[128,640]{1,0:T(8,128)(2,1)}, u32[]{:S(2)}) copy-start(bf16[128,640]{1,0:T(8,128)(2,1)} %copy-done.17) | copy-start | bytes 491524
  118.5 5.5 %copy-start.26 = (bf16[128,640]{1,0:T(8,128)(2,1)S(1)}, bf16[128,640]{1,0:T(8,128)(2,1)}, u32[]{:S(2)}) copy-start(bf16[128,640]{1,0:T(8,128)(2,1)} %copy-done.25) | copy-start | bytes 491524
  126.4 95.7 %copy-start.29 = (f32[128,128]{1,0:T(8,128)S(1)}, f32[128,128]{1,0:T(8,128)}, u32[]{:S(2)}) copy-start(f32[128,128]{1,0:T(8,128)} %copy-done.28) | copy-start | bytes 196612
  126.4 95.7 %copy-start.31 = (f32[128,128]{1,0:T(8,128)S(1)}, f32[128,128]{1,0:T(8,128)}, u32[]{:S(2)}) copy-start(f32[128,128]{1,0:T(8,128)} %copy-done.30) | copy-start | bytes 196612
  126.4 95.7 %copy-start.45 = (f32[1,256]{1,0:T(1,128)S(1)}, f32[1,256]{1,0:T(1,128)}, u32[]{:S(2)}) copy-start(f32[1,256]{1,0:T(1,128)} %copy-done.44) | copy-start | bytes 3076
  126.4 95.7 %copy-start.55 = (f32[128]{0:T(128)S(1)}, f32[128]{0:T(128)}, u32[]{:S(2)}) copy-start(f32[128]{0:T(128)} %copy-done.54) | copy-start | bytes 1540
  126.4 96.9 %copy-start.39 = (f32[4,128]{0,1:T(8,128)S(1)}, f32[4,128]{0,1:T(8,128)}, u32[]{:S(2)}) copy-start(f32[4,128]{0,1:T(8,128)} %get-tuple-element.29) | copy-start | bytes 6148
  126.4 96.9 %copy-start.15 = (f32[4,128,256]{2,0,1:T(4,128)S(1)}, f32[4,128,256]{2,0,1:T(4,128)}, u32[]{:S(2)}) copy-start(f32[4,128,256]{2,0,1:T(4,128)} %get-tuple-element.44) | copy-start | bytes 1572868
  221.0 4.7 %copy-start = (bf16[640,1536]{1,0:T(8,128)(2,1)S(1)}, bf16[640,1536]{1,0:T(8,128)(2,1)}, u32[]{:S(2)}) copy-start(bf16[640,1536]{1,0:T(8,128)(2,1)} %shard_map.152) | copy-start | bytes 5898244
  221.0 4.7 %copy-start.9 = (bf16[1,128,640]{2,1,0:T(8,128)(2,1)S(1)}, bf16[1,128,640]{2,1,0:T(8,128)(2,1)}, u32[]{:S(2)}) copy-start(bf16[1,128,640]{2,1,0:T(8,128)(2,1)} %param.9) | copy-start | bytes 491524
  221.0 4.7 %copy-start.57 = (f32[128]{0:T(128)S(1)}, f32[128]{0:T(128)}, u32[]{:S(2)}) copy-start(f32[128]{0:T(128)} %copy-done.56) | copy-start | bytes 1540
  223.6 2.9 %copy-start.51 = (f32[640]{0:T(1024)S(1)}, f32[640]{0:T(1024)}, u32[]{:S(2)}) copy-start(f32[640]{0:T(1024)} %get-tuple-element.34) | copy-start | bytes 7684
  223.7 2.9 %copy-start.58 = (f32[640]{0:T(1024)S(1)}, f32[640]{0:T(1024)}, u32[]{:S(2)}) copy-start(f32[640]{0:T(1024)} %get-tuple-element.32) | copy-start | bytes 7684
  223.7 2.9 %copy-start.50 = (f32[640]{0:T(1024)S(1)}, f32[640]{0:T(1024)}, u32[]{:S(2)}) copy-start(f32[640]{0:T(1024)} %get-tuple-element.36) | copy-start | bytes 7684
  229.3 44.0 %copy-start.11 = (f32[128,640]{1,0:T(8,128)S(1)}, f32[128,640]{1,0:T(8,128)}, u32[]{:S(2)}) copy-start(f32[128,640]{1,0:T(8,128)} %copy-done.10) | copy-start | bytes 983044
  229.3 44.8 %copy-start.19 = (bf16[160,4096]{1,0:T(8,128)(2,1)S(1)}, bf16[160,4096]{1,0:T(8,128)(2,1)}, u32[]{:S(2)}) copy-start(bf16[160,4096]{1,0:T(8,128)(2,1)} %get-tuple-element.25) | copy-start | bytes 3932164
  274.1 1.8 copy-start.27
  274.1 2.9 %copy-start.38 = (bf16[256,640]{1,0:T(8,128)(2,1)S(1)}, bf16[256,640]{1,0:T(8,128)(2,1)}, u32[]{:S(2)}) copy-start(bf16[256,640]{1,0:T(8,128)(2,1)} %get-tuple-element.24) | copy-start | bytes 983044

commit v3 on v2

--- a/solution.py
+++ b/solution.py
@@ -198,7 +198,7 @@
         step = 1024 if width % 1024 == 0 else 768 if width % 768 == 0 else width
         plan += [(index, col, step) for col in range(0, width, step)]
     count = len(arrays)
-    assert len(plan) + 2 >= zn - 1
+    assert len(plan) + 2 >= (zn - 1) * len(kv)
     shapes = [((4 * array.shape[0], array.shape[1]), array.dtype) for array in arrays]
     shapes += [((2 * zn,) + block.shape, block.dtype) for block in kv]
     copies = 5 * len(plan) + len(kv) * (2 * zn - 1)
@@ -467,7 +467,8 @@
     all_places = positions[0]
     length = all_places.shape[0]
     places = lax.dynamic_slice_in_dim(all_places, lax.axis_index("ctx") * row_count, row_count, 0)
-    weights = (out_weight, down_weight, gate_up_weight)
+    weights = (out_weight, down_weight)
+    gate_up_full = lax.all_gather(gate_up_weight, "fsdp", axis=0, tiled=True)
     if own_kernels:
         (qkv_full,) = gather_weights((qkv_weight,), (), zn)
     else:
@@ -492,10 +493,10 @@
     key_b = rotate(key_norm, cosine, sine_part).astype(BF)
     kv_b = jnp.concatenate([key_b, value_b], 1)
     if own_kernels:
-        out_full, down_full, gate_up_full, kv_all = gather_weights(weights, (kv_b,), zn)
+        out_full, down_full, kv_all = gather_weights(weights, (kv_b,), zn)
         kv_all = kv_all.reshape(length, 2 * head_size)
     else:
-        out_full, down_full, gate_up_full = [
+        out_full, down_full = [
             lax.all_gather(weight, "fsdp", axis=0, tiled=True) for weight in weights
         ]
         kv_all = lax.all_gather(kv_b, "ctx", axis=0, tiled=True)

time: 279 us -> 281 us (level)
  between operations: 1.64 us -> 14.8 us
  Pallas kernels: 211 us -> 200 us
  other arithmetic: 23.4 us -> 18.7 us
    pallas_call x2, Pallas kernels: 76.7 us -> 65.6 us  [gather_weights(): pl.pallas_call(functools.partial(gather_kernel, plan, count, len(kv), zn)...]
  transfers between devices with their start and end apart: 0 -> 1, of which waited for: 0 -> 0; matrix products, arithmetic and copies ran while one was open for 0% -> 4% of each run, Pallas kernels for 0% -> 23%
where the time goes in v3:
time: 281 us; the launch traced here: 280 us
  Pallas kernels  200 us (71%)
  matrix products  33.7 us (12%)
  other arithmetic  18.7 us (7%)
  between operations  14.8 us (5%)
  local copies, waits for them, and re-layouts  12.8 us (5%)
    pallas_call x2, Pallas kernels, reduce_weights(): pl.pallas_call(functools.partial(reduce_kernel, plan, count, with_kv, zn)...  134 us
    pallas_call x2, Pallas kernels, gather_weights(): pl.pallas_call(functools.partial(gather_kernel, plan, count, len(kv), zn)...  65.6 us
    dot_general x6, matrix products, tn(): lax.dot_general(left, right, (((0,), (0,)), ((), ())), preferred_element_...  13.2 us
    dot_general x6, matrix products, nn(): return jnp.dot(left, right, preferred_element_type=F32)  11 us
    dot_general x6, matrix products, nt(): lax.dot_general(left, right, (((1,), (1,)), ((), ())), preferred_element_...  9.45 us
  transfers between devices with their start and end apart: 1, of which 0 were waited for; matrix products, arithmetic and copies ran while one was open for 4% of the time, Pallas kernels for 23%

profile of v3, /device:TPU:0, one launch (start us, length us, event | category | flops | bytes accessed | tf_op | source)
XLA Modules:
  0.0 280.4 jit_solution(3606074851983053527)
XLA Ops:
  7.2 0.7 all-gather.2.cloned.1.call-update
  7.9 20.3 %shard_map.152 = bf16[640,1536]{1,0:T(8,128)(2,1)} custom-call(bf16[160,1536]{1,0:T(8,128)(2,1)} %refs_0_.2), custom_call_target="tpu_custom_call" | custom-call | tf_op jit(solution)/shard_map/pallas_call | solution.py:205
  28.5 2.1 fusion.56
  30.6 0.2 reshape.187
  31.1 0.2 fusion.24
  31.4 0.3 multiply_cosine_fusion
  31.8 0.7 broadcast_multiply_fusion
  32.5 0.2 fusion.37
  32.7 0.1 slice_negate_fusion.1
  32.8 0.3 fusion.22
  33.3 0.7 pad_maximum_fusion.9.refs_2_
  34.0 45.2 %shard_map.153 = (bf16[1024,640]{1,0:T(8,128)(2,1)}, bf16[2048,640]{1,0:T(8,128)(2,1)}, bf16[8,128,512]{2,1,0:T(8,128)(2,1)}) custom-call(bf16[256,640]{1,0:T(8,128)(2,1)} %refs_0_.3, bf16[512,640]{1,0:T(8,128)(2,1)} %refs_1_.1, bf16[128,512]{1,0:T(8,128)(2,1)} %pad_maximum_fusion.9.refs_2_), custom_call_target="tpu_custom_call" | custom-call | tf_op jit(solution)/shard_map/pallas_call | solution.py:205
  79.2 1.7 fusion.5
  80.9 0.6 exponential_reduce_fusion
  81.5 0.6 convolution_convert_fusion.7
  82.2 0.2 copy.24
  82.3 0.5 copy-done.15
  82.8 1.8 multiply_reduce_fusion.9
  84.7 0.2 multiply_reduce_fusion.8
  84.9 3.5 %fusion.65 = f32[128,4096]{1,0:T(8,128)S(1)} fusion(bf16[640,4096]{1,0:T(8,128)(2,1)} %all-gather.2.cloned.1.call-done, f32[128,640]{1,0:T(8,128)S(1)} %get-tuple-element.46, f32[640]{0:T(1024)S(1)} %get-tuple-element.41, f32[128]{0:T(128)S(1)} %add_rsqrt_fusion.2), kind=kOutput, calls=%fused_computation.154 | convolution fusion | flops 671334400 | bytes 7670784 | tf_op jit(solution)/shard_map/dot_general | solution.py:61
  88.5 0.4 multiply_convert_fusion.2
  88.8 1.3 copy-done.6
  90.2 0.7 multiply_reduce_fusion.7
  90.9 0.2 fusion.49
  91.1 0.9 fusion.40
  92.0 1.4 fusion.12
  93.4 3.9 %convolution_convert_fusion.refs_2_ = bf16[640,4096]{1,0:T(8,128)(2,1)} fusion(bf16[128,2048]{1,0:T(8,128)(2,1)S(1)} %get-tuple-element.50, bf16[128,2048]{1,0:T(8,128)(2,1)S(1)} %get-tuple-element.49, f32[128,640]{1,0:T(8,128)S(1)} %get-tuple-element.46, f32[640]{0:T(1024)S(1)} %get-tuple-element.41, f32[128]{0:T(128)S(1)} %add_rsqrt_fusion.2), kind=kOutput, calls=%fused_computation | convolution fusion | flops 676052992 | bytes 6622208 | tf_op jit(solution)/shard_map/dot_general | solution.py:57
  97.4 2.4 multiply_reduce_fusion.3
  99.7 0.3 multiply_reduce_fusion.4
  100.1 0.7 copy-done.4
  100.8 0.1 multiply_convert_fusion.5
  100.9 0.3 copy-done.2
  101.2 0.5 convolution_convert_fusion.6
  101.7 1.5 convolution_convert_fusion.3.refs_1_
  103.3 2.4 convolution_convert_fusion.2.refs_0_
  105.7 0.2 multiply_reduce_fusion.2
  105.9 2.6 fusion
  108.5 2.3 copy.30
  110.8 2.4 copy.31
  113.2 1.7 convolution_convert_fusion.5
  114.8 1.7 convolution_convert_fusion.4
  116.5 1.1 pad_maximum_fusion.1.refs_3_
  117.6 95.0 %shard_map.154 = (bf16[512,640]{1,0:T(8,128)(2,1)}, bf16[256,640]{1,0:T(8,128)(2,1)}, bf16[160,4096]{1,0:T(8,128)(2,1)}, f32[128,512]{1,0:T(8,128)}) custom-call(bf16[2048,640]{1,0:T(8,128)(2,1)} %convolution_convert_fusion.2.refs_0_, bf16[1024,640]{1,0:T(8,128)(2,1)} %convolution_convert_fusion.3.refs_1_, ...), custom_call_target="tpu_custom_call" | custom-call | tf_op jit(solution)/shard_map/pallas_call | solution.py:431
  212.6 0.9 slice_negate_fusion.3
  213.5 0.9 slice.168
  214.4 2.4 fusion.18
  216.9 0.4 copy_multiply_fusion
  217.2 0.1 slice_negate_fusion
  217.4 0.4 copy-done.22
  217.8 0.9 multiply_reduce_fusion
  218.7 0.4 multiply_convert_fusion.4
  219.2 1.2 multiply_reduce_fusion.10
  220.4 1.0 multiply_convert_fusion.7
  221.4 0.8 fusion.47
  222.3 2.0 convolution_convert_fusion.1.refs_0_
  224.4 0.6 concatenate.51.refs_1_
  225.0 39.1 %shard_map.155 = (bf16[160,1536]{1,0:T(8,128)(2,1)}, f32[8,640]{1,0:T(8,128)}) custom-call(bf16[640,1536]{1,0:T(8,128)(2,1)} %convolution_convert_fusion.1.refs_0_, f32[8,640]{1,0:T(8,128)} %concatenate.51.refs_1_), custom_call_target="tpu_custom_call" | custom-call | tf_op jit(solution)/shard_map/pallas_call | solution.py:431
  264.1 1.3 slice.108
  265.5 1.3 slice.109
  266.7 2.1 convert_element_type.119
  268.8 1.8 convert_element_type.121
  270.6 1.1 convert_element_type.122
  271.8 0.9 convert_element_type.120
  272.6 0.9 fusion.46
  (101 shorter events, 0.9 us)
Async XLA Ops:
  7.2 21.1 %copy-start.27 = (f32[4,640]{1,0:T(4,128)S(1)}, f32[4,640]{1,0:T(4,128)}, u32[]{:S(2)}) copy-start(f32[4,640]{1,0:T(4,128)} %param.15) | copy-start | bytes 30724
  7.2 21.2 %copy-start.3 = (bf16[1,128,640]{2,1,0:T(8,128)(2,1)S(1)}, bf16[1,128,640]{2,1,0:T(8,128)(2,1)}, u32[]{:S(2)}) copy-start(bf16[1,128,640]{2,1,0:T(8,128)(2,1)} %param.9) | copy-start | bytes 491524
  7.2 77.7 %all-gather.2.cloned.1.call-start = ((), (), s32[]{:S(2)}) async-start(), calls=%async_computation | async-start | bytes 6553600 | tf_op jit(solution)/shard_map/all_gather | solution.py:471
  28.5 2.4 copy-start.30
  28.5 2.5 copy-start.26
  30.5 2.0 copy-start.1
  30.6 0.7 copy-start.33
  31.8 1.5 copy-start.18
  31.8 1.5 copy-start.20
  33.3 47.7 %copy-start.13 = (bf16[4,128,256]{2,1,0:T(8,128)(2,1)}, bf16[4,128,256]{2,1,0:T(8,128)(2,1)S(1)}, u32[]{:S(2)}) copy-start(bf16[4,128,256]{2,1,0:T(8,128)(2,1)S(1)} %copy.23) | copy-start | bytes 786436
  79.2 2.3 copy-start.11
  82.2 0.7 copy-start.15
  82.3 2.3 copy-start.7
  84.6 3.8 %copy-start.28 = (f32[128]{0:T(128)}, f32[128]{0:T(128)S(1)}, u32[]{:S(2)}) copy-start(f32[128]{0:T(128)S(1)} %add_rsqrt_fusion.3) | copy-start | bytes 1540
  88.4 1.7 copy-start.6
  88.8 2.0 copy-start.9
  91.1 6.2 %slice-start = ((s8[5242880]{0:T(1024)(128)(4,1)}), s8[4194304]{0:T(1024)(128)(4,1)S(1)}, s32[]{:S(2)}) async-start(s8[5242880]{0:T(1024)(128)(4,1)} %bitcast.107), calls=%async_computation.1 | async-start | bytes 8388608
  92.0 5.3 %slice-start.1 = ((s8[5242880]{0:T(1024)(128)(4,1)}), s8[1048576]{0:T(1024)(128)(4,1)S(1)}, s32[]{:S(2)}) async-start(s8[5242880]{0:T(1024)(128)(4,1)} %bitcast.107), calls=%async_computation.2 | async-start | bytes 2097152
  97.4 2.4 copy-start.29
  99.7 1.4 copy-start.2
  99.7 2.0 copy-start.8
  100.0 0.7 copy-start.4
  103.3 2.4 copy-start.16
  103.3 2.6 copy-start.12
  108.5 4.7 %copy-start.14 = (bf16[4,128,256]{2,1,0:T(8,128)(2,1)S(1)}, bf16[4,128,256]{2,1,0:T(8,128)(2,1)}, u32[]{:S(2)}) copy-start(bf16[4,128,256]{2,1,0:T(8,128)(2,1)} %copy-done.13) | copy-start | bytes 786436
  216.8 0.9 copy-start.22
  216.8 1.0 copy-start.23
  217.8 1.3 copy-start.19
  217.8 1.3 copy-start.21
  217.8 1.3 copy-start.24
  218.7 2.7 copy-start
  218.7 2.7 copy-start.31
  222.3 2.1 copy-start.32
  224.3 44.5 %copy-start.10 = (bf16[160,4096]{1,0:T(8,128)(2,1)S(1)}, bf16[160,4096]{1,0:T(8,128)(2,1)}, u32[]{:S(2)}) copy-start(bf16[160,4096]{1,0:T(8,128)(2,1)} %get-tuple-element.23) | copy-start | bytes 3932164
  268.8 1.8 copy-start.17
  268.8 2.9 %copy-start.25 = (bf16[256,640]{1,0:T(8,128)(2,1)S(1)}, bf16[256,640]{1,0:T(8,128)(2,1)}, u32[]{:S(2)}) copy-start(bf16[256,640]{1,0:T(8,128)(2,1)} %get-tuple-element.22) | copy-start | bytes 983044
  270.6 2.0 copy-start.5
Sparse Core Ops, SparseCore 0:
  9.6 53.7 all-gather.1
